TPU v7x, 32 devices: a whole 2x2x4 slice. The times are simulated.
32 devices in a mesh: fsdp: 32 (over z, y, x, core).
Axes of the slice: x: 2, y: 2, z: 4, core: 2. Of those that a mesh axis runs over, the one named last changes fastest.
Arguments:
- inputs: bfloat16 [2, 16384, 1024], P(None, 'fsdp'), may hold values from -6 to 6
- segments: int32 [2, 16384], P(None, 'fsdp'), may hold values from 0 to 24, as said below
- attn_gain: bfloat16 [1024], P('fsdp'), may hold values from 0.5 to 1.5
- w_query: bfloat16 [1024, 1024], P('fsdp'), may hold values from -0.1875 to 0.1875
- key_projection: bfloat16 [1024, 512], P('fsdp'), may hold values from -0.1875 to 0.1875
- value_projection: bfloat16 [1024, 512], P('fsdp'), may hold values from -0.1875 to 0.1875
- w_output: bfloat16 [1024, 1024], P(None, 'fsdp'), may hold values from -1 to 1
- query_gain: bfloat16 [64], replicated, may hold values from 0.5 to 1.5
- key_norm_gain: bfloat16 [64], replicated, may hold values from 0.5 to 1.5
- ffn_gain: bfloat16 [1024], P('fsdp'), may hold values from 0.5 to 1.5
- w_gate: bfloat16 [1024, 4608], P('fsdp'), may hold values from -0.1875 to 0.1875
- w_up: bfloat16 [1024, 4608], P('fsdp'), may hold values from -0.1875 to 0.1875
- w_down: bfloat16 [4608, 1024], P(None, 'fsdp'), may hold values from -0.09375 to 0.09375
- cotangent: bfloat16 [2, 16384, 1024], P(None, 'fsdp'), may hold values from -6 to 6
Outputs:
- outputs: bfloat16 [2, 16384, 1024], P(None, 'fsdp')
- input_grad: bfloat16 [2, 16384, 1024], P(None, 'fsdp')
- attn_gain_grad: float32 [1024], P('fsdp')
- w_query_grad: float32 [1024, 1024], P('fsdp')
- w_key_grad: float32 [1024, 512], P('fsdp')
- w_value_grad: float32 [1024, 512], P('fsdp')
- w_output_grad: float32 [1024, 1024], P(None, 'fsdp')
- query_gain_grad: float32 [64], replicated
- key_gain_grad: float32 [64], replicated
- ffn_gain_grad: float32 [1024], P('fsdp')
- w_gate_grad: float32 [1024, 4608], P('fsdp')
- w_up_grad: float32 [1024, 4608], P('fsdp')
- w_down_grad: float32 [4608, 1024], P(None, 'fsdp')
Inputs may be any that keep to these rules, and one draw needn't show every extreme that they name: `segments`: within each sequence of 1024 tokens beginning at a multiple of 1024 along a micro-batch, the numbers start at 0, never fall, and are 24 at the sequence's last token; a document is a maximal stretch of one number inside a sequence.
All inputs are finite; a program needn't handle non-finite values.
Results may differ from a plain program's by a relative error of at most 0.013.
Values may be sent and summed in bfloat16 or wider, within the bound.
A program may use at most 320 MiB of HBM per device.

v0:
```python
import math

import jax
import jax.numpy as jnp
from jax import lax
from jax.sharding import PartitionSpec as P

SEQ = 1024


EPS = 1e-05
THETA = 1000000.0
NEG = -1e30


def from_behind(block, axis, distance):
    devices = range(lax.axis_size(axis))
    route = [(i - distance, i) for i in devices if i - distance in devices]
    return lax.ppermute(block, axis, route)


def row_norm(values, gain_row):
    return values * lax.rsqrt(jnp.mean(values * values, axis=-1, keepdims=True) + EPS) * gain_row


def angles(places, head_width):
    counter = jnp.arange(head_width // 2, dtype=jnp.float32)
    inverse = jnp.power(jnp.float32(THETA), -2.0 * counter / head_width)
    turned = places.astype(jnp.float32)[:, None] * inverse[None, :]
    return (jnp.cos(turned), jnp.sin(turned))


def prepare_inputs(raw_rows, gain_row, cosine_table, sine_table_rows, head_count):
    token_count = raw_rows.shape[0]
    head_width = gain_row.shape[0]
    split_rows = raw_rows.reshape(token_count, head_count, head_width)
    normed = row_norm(split_rows, gain_row)
    first_half = normed[..., : head_width // 2]
    second = normed[..., head_width // 2 :]
    cos_rows = cosine_table[:, None, :]
    sin_rows = sine_table_rows[:, None, :]
    turned = jnp.concatenate(
        [first_half * cos_rows - second * sin_rows, second * cos_rows + first_half * sin_rows],
        axis=-1,
    )
    return turned.reshape(token_count, head_count * head_width)


def plain_product(left_rows, right_rows):
    return jnp.dot(left_rows, right_rows, preferred_element_type=jnp.float32)


def rows_product(left_rows, right_rows):
    return lax.dot_general(
        left_rows, right_rows, (((0,), (0,)), ((), ())), preferred_element_type=jnp.float32
    )


def cols_product(left_rows, right_rows):
    return lax.dot_general(
        left_rows, right_rows, (((1,), (1,)), ((), ())), preferred_element_type=jnp.float32
    )


def silu_product(gate_raw, upward):
    return gate_raw * jax.nn.sigmoid(gate_raw) * upward


def add_sets(former_set, latter_set):
    if former_set is None:
        return latter_set
    return tuple((former + latter for former, latter in zip(former_set, latter_set)))


def local(
    inputs,
    segments,
    attn_gain,
    w_query,
    key_projection,
    value_projection,
    w_output,
    query_gain,
    key_norm_gain,
    ffn_gain,
    w_gate,
    w_up,
    w_down,
    cotangent,
):
    batches = inputs.shape[0]
    tokens = inputs.shape[1]
    head_width = query_gain.shape[0]
    query_width = w_query.shape[1]
    kv_width = key_projection.shape[1]
    query_head_rows = query_width // head_width
    kv_heads = kv_width // head_width
    heads_per_group = query_head_rows // kv_heads
    scale = 1.0 / math.sqrt(head_width)
    query_gain_f = query_gain.astype(jnp.float32)
    key_gain_f = key_norm_gain.astype(jnp.float32)
    device_index = lax.axis_index("fsdp")
    places_row = jnp.arange(tokens, dtype=jnp.int32)
    causal = places_row[None, :] <= places_row[:, None]
    same_run = device_index * tokens // SEQ == (device_index - 1) * tokens // SEQ
    outputs_list = []
    grads_list = []
    shard_sums = None
    gain_sums = None
    for batch_index in range(batches):
        gathered = (
            lax.all_gather(attn_gain, "fsdp", axis=0, tiled=True),
            lax.all_gather(w_query, "fsdp", axis=0, tiled=True),
            lax.all_gather(key_projection, "fsdp", axis=0, tiled=True),
            lax.all_gather(value_projection, "fsdp", axis=0, tiled=True),
            lax.all_gather(w_output, "fsdp", axis=1, tiled=True),
            lax.all_gather(ffn_gain, "fsdp", axis=0, tiled=True),
            lax.all_gather(w_gate, "fsdp", axis=0, tiled=True),
            lax.all_gather(w_up, "fsdp", axis=0, tiled=True),
            lax.all_gather(w_down, "fsdp", axis=1, tiled=True),
        )
        (
            gain_attn,
            full_query,
            full_key,
            full_value,
            full_output,
            gain_ffn,
            full_gate,
            full_up,
            full_down,
        ) = gathered
        hidden = inputs[batch_index].astype(jnp.float32)
        segment = segments[batch_index]
        normed_f, norm_pull = jax.vjp(row_norm, hidden, gain_attn.astype(jnp.float32))
        normed = normed_f.astype(jnp.bfloat16)
        query_raw = plain_product(normed, full_query)
        key_projected = plain_product(normed, full_key)
        value_reduced = plain_product(normed, full_value).astype(jnp.bfloat16)
        lower_count = jnp.sum((segment[None, :] < segment[:, None]).astype(jnp.int32), axis=1)
        local_places = places_row - lower_count
        cos_local, sin_local = angles(local_places, head_width)
        key_sent = prepare_inputs(key_projected, key_gain_f, cos_local, sin_local, kv_heads).astype(
            jnp.bfloat16
        )
        remote_key, remote_value, remote_segment = from_behind(
            (key_sent, value_reduced, segment.astype(jnp.bfloat16)), "fsdp", 1
        )
        remote_match = (remote_segment.astype(jnp.int32)[None, :] == segment[:, None]) & same_run
        places_all = local_places + jnp.sum(remote_match.astype(jnp.int32), axis=1)
        cosine_table, sine_table_rows = angles(places_all, head_width)
        query_f, query_pull = jax.vjp(
            lambda raw_rows, gain_row: prepare_inputs(
                raw_rows, gain_row, cosine_table, sine_table_rows, query_head_rows
            ),
            query_raw,
            query_gain_f,
        )
        key_f, key_pull = jax.vjp(
            lambda raw_rows, gain_row: prepare_inputs(
                raw_rows, gain_row, cosine_table, sine_table_rows, kv_heads
            ),
            key_projected,
            key_gain_f,
        )
        query_low = query_f.astype(jnp.bfloat16)
        key_low = key_f.astype(jnp.bfloat16)
        allowed = jnp.concatenate(
            [remote_match, causal & (segment[None, :] == segment[:, None])], axis=1
        )
        query_split = query_low.reshape(tokens, kv_heads, heads_per_group, head_width).transpose(
            1, 0, 2, 3
        )
        key_split = (
            jnp.concatenate([remote_key, key_low], axis=0)
            .reshape(2 * tokens, kv_heads, head_width)
            .transpose(1, 0, 2)
        )
        value_split = (
            jnp.concatenate([remote_value, value_reduced], axis=0)
            .reshape(2 * tokens, kv_heads, head_width)
            .transpose(1, 0, 2)
        )

        def head_forward(blocks):
            query_part, key_part, value_part = blocks
            scores = (
                jnp.einsum("tgd,ld->gtl", query_part, key_part, preferred_element_type=jnp.float32)
                * scale
            )
            scores = jnp.where(allowed[None], scores, NEG)
            row_peak = jnp.max(scores, axis=-1, keepdims=True)
            raised = jnp.exp(scores - row_peak)
            row_total = jnp.sum(raised, axis=-1, keepdims=True)
            prob_rows = (raised / row_total).astype(jnp.bfloat16)
            mixed_part = jnp.einsum(
                "gtl,ld->tgd", prob_rows, value_part, preferred_element_type=jnp.float32
            )
            return (mixed_part.astype(jnp.bfloat16), (row_peak + jnp.log(row_total))[..., 0])

        mixed_split, log_totals = lax.map(head_forward, (query_split, key_split, value_split))
        attn_mix = mixed_split.transpose(1, 0, 2, 3).reshape(tokens, query_width)
        attended = hidden + plain_product(attn_mix, full_output)
        ffn_f, ffn_pull = jax.vjp(row_norm, attended, gain_ffn.astype(jnp.float32))
        ffn_in = ffn_f.astype(jnp.bfloat16)
        gate_raw = plain_product(ffn_in, full_gate)
        upward = plain_product(ffn_in, full_up)
        active_f, active_pull = jax.vjp(silu_product, gate_raw, upward)
        active = active_f.astype(jnp.bfloat16)
        result = attended + plain_product(active, full_down)
        outputs_list.append(result.astype(jnp.bfloat16))
        back_query, back_key, back_value, back_output, back_gate, back_up, back_down = (
            lax.all_gather(w_query, "fsdp", axis=0, tiled=True),
            lax.all_gather(key_projection, "fsdp", axis=0, tiled=True),
            lax.all_gather(value_projection, "fsdp", axis=0, tiled=True),
            lax.all_gather(w_output, "fsdp", axis=1, tiled=True),
            lax.all_gather(w_gate, "fsdp", axis=0, tiled=True),
            lax.all_gather(w_up, "fsdp", axis=0, tiled=True),
            lax.all_gather(w_down, "fsdp", axis=1, tiled=True),
        )
        grad_result = cotangent[batch_index]
        grad_down_t = rows_product(grad_result, active)
        grad_active = cols_product(grad_result, back_down)
        grad_gate_f, grad_up_f = active_pull(grad_active)
        grad_gate_low = grad_gate_f.astype(jnp.bfloat16)
        grad_up_low = grad_up_f.astype(jnp.bfloat16)
        grad_gate_w = rows_product(ffn_in, grad_gate_low)
        grad_up_w = rows_product(ffn_in, grad_up_low)
        grad_ffn_in = cols_product(grad_gate_low, back_gate) + cols_product(grad_up_low, back_up)
        grad_attended_norm, grad_ffn_gain = ffn_pull(grad_ffn_in)
        grad_attended = grad_result.astype(jnp.float32) + grad_attended_norm
        grad_branch = grad_attended.astype(jnp.bfloat16)
        grad_output_t = rows_product(grad_branch, attn_mix)
        grad_mixed = cols_product(grad_branch, back_output).astype(jnp.bfloat16)
        grad_split = grad_mixed.reshape(tokens, kv_heads, heads_per_group, head_width).transpose(
            1, 0, 2, 3
        )

        def head_backward(blocks):
            query_part, key_part, value_part, grad_part, log_part = blocks
            scores = (
                jnp.einsum("tgd,ld->gtl", query_part, key_part, preferred_element_type=jnp.float32)
                * scale
            )
            scores = jnp.where(allowed[None], scores, NEG)
            prob_rows = jnp.exp(scores - log_part[..., None])
            grad_probs = jnp.einsum(
                "tgd,ld->gtl", grad_part, value_part, preferred_element_type=jnp.float32
            )
            center = jnp.sum(prob_rows * grad_probs, axis=-1, keepdims=True)
            grad_scores = (prob_rows * (grad_probs - center)).astype(jnp.bfloat16)
            grad_query_part = (
                jnp.einsum("gtl,ld->tgd", grad_scores, key_part, preferred_element_type=jnp.float32)
                * scale
            )
            grad_key_part = (
                jnp.einsum(
                    "gtl,tgd->ld", grad_scores, query_part, preferred_element_type=jnp.float32
                )
                * scale
            )
            grad_value_part = jnp.einsum(
                "gtl,tgd->ld",
                prob_rows.astype(jnp.bfloat16),
                grad_part,
                preferred_element_type=jnp.float32,
            )
            return (grad_query_part, grad_key_part, grad_value_part)

        grad_query_split, grad_key_split, grad_value_split = lax.map(
            head_backward, (query_split, key_split, value_split, grad_split, log_totals)
        )
        grad_query_rot = grad_query_split.transpose(1, 0, 2, 3).reshape(tokens, query_width)
        grad_key_all = grad_key_split.transpose(1, 0, 2).reshape(2 * tokens, kv_width)
        grad_value_all = grad_value_split.transpose(1, 0, 2).reshape(2 * tokens, kv_width)
        back_key_grad, back_value_grad = (
            from_behind(grad_key_all[:tokens].astype(jnp.bfloat16), "fsdp", -1).astype(jnp.float32),
            from_behind(grad_value_all[:tokens].astype(jnp.bfloat16), "fsdp", -1).astype(
                jnp.float32
            ),
        )
        grad_key_rot = grad_key_all[tokens:] + back_key_grad
        grad_value_low = (grad_value_all[tokens:] + back_value_grad).astype(jnp.bfloat16)
        grad_query_raw, grad_query_gain = query_pull(grad_query_rot)
        grad_key_raw, grad_key_gain = key_pull(grad_key_rot)
        grad_query_low = grad_query_raw.astype(jnp.bfloat16)
        grad_key_low = grad_key_raw.astype(jnp.bfloat16)
        grad_query_w = rows_product(normed, grad_query_low)
        grad_key_w = rows_product(normed, grad_key_low)
        grad_value_w = rows_product(normed, grad_value_low)
        grad_normed = (
            cols_product(grad_query_low, back_query)
            + cols_product(grad_key_low, back_key)
            + cols_product(grad_value_low, back_value)
        )
        grad_hidden_norm, grad_attn_gain = norm_pull(grad_normed)
        grads_list.append((grad_attended + grad_hidden_norm).astype(jnp.bfloat16))
        gain_sums = add_sets(gain_sums, (grad_query_gain, grad_key_gain))
        shard_terms = (
            lax.psum_scatter(grad_attn_gain, "fsdp", scatter_dimension=0, tiled=True),
            lax.psum_scatter(grad_query_w, "fsdp", scatter_dimension=0, tiled=True),
            lax.psum_scatter(grad_key_w, "fsdp", scatter_dimension=0, tiled=True),
            lax.psum_scatter(grad_value_w, "fsdp", scatter_dimension=0, tiled=True),
            lax.psum_scatter(grad_output_t, "fsdp", scatter_dimension=0, tiled=True),
            lax.psum_scatter(grad_ffn_gain, "fsdp", scatter_dimension=0, tiled=True),
            lax.psum_scatter(grad_gate_w, "fsdp", scatter_dimension=0, tiled=True),
            lax.psum_scatter(grad_up_w, "fsdp", scatter_dimension=0, tiled=True),
            lax.psum_scatter(grad_down_t, "fsdp", scatter_dimension=0, tiled=True),
        )
        shard_sums = add_sets(shard_sums, shard_terms)
    head_sums = lax.psum((gain_sums[0], gain_sums[1]), "fsdp")
    return (
        jnp.stack(outputs_list),
        jnp.stack(grads_list),
        shard_sums[0],
        shard_sums[1],
        shard_sums[2],
        shard_sums[3],
        shard_sums[4].T,
        head_sums[0],
        head_sums[1],
        shard_sums[5],
        shard_sums[6],
        shard_sums[7],
        shard_sums[8].T,
    )


def solution(mesh):
    return jax.shard_map(
        local,
        mesh=mesh,
        in_specs=(
            P(None, "fsdp", None),
            P(None, "fsdp"),
            P("fsdp"),
            P("fsdp", None),
            P("fsdp", None),
            P("fsdp", None),
            P(None, "fsdp"),
            P(),
            P(),
            P("fsdp"),
            P("fsdp", None),
            P("fsdp", None),
            P(None, "fsdp"),
            P(None, "fsdp", None),
        ),
        out_specs=(
            P(None, "fsdp", None),
            P(None, "fsdp", None),
            P("fsdp"),
            P("fsdp", None),
            P("fsdp", None),
            P("fsdp", None),
            P(None, "fsdp"),
            P(),
            P(),
            P("fsdp"),
            P("fsdp", None),
            P("fsdp", None),
            P(None, "fsdp"),
        ),
        check_vma=False,
    )
```

profile of v0, /device:TPU:0, one launch (start us, length us, event | category | flops | bytes accessed | tf_op | source)
XLA Modules:
  0.0 2040.1 jit_solution(215551554843041505)
XLA Ops:
  14.4 4.5 collective-permute-start.1
  22.1 40.5 %all-reduce.13 = (bf16[1024]{0:T(1024)(128)(2,1)S(1)}, bf16[1024]{0:T(1024)(128)(2,1)S(1)}) all-reduce(bf16[1024]{0:T(1024)(128)(2,1)S(1)} %dynamic-update-slice, bf16[1024]{0:T(1024)(128)(2,1)S(1)} %dynamic-update-slice.1), channel_id=1, replica_groups=mesh['fsdp'=32] {'fsdp'}, use_global_device_ids=true, to_apply=%add.8 | all-reduce | flops 2048 | bytes 8192
  73.1 49.8 %all-gather.10.cloned.1.call-done = bf16[1024,512]{1,0:T(8,128)(2,1)} async-done(((bf16[32,512]{1,0:T(8,128)(2,1)}), bf16[1024,512]{1,0:T(8,128)(2,1)}) %all-gather.10.cloned.1.call-update) | async-done | bytes 1048592 | tf_op jit(solution)/shard_map/all_gather | solution.py:114
  157.6 25.8 %all-gather.12.cloned.1.call-done = bf16[1024,1024]{1,0:T(8,128)(2,1)} async-done(((bf16[32,1024]{1,0:T(8,128)(2,1)}), bf16[1024,1024]{1,0:T(8,128)(2,1)}) %all-gather.12.cloned.1.call-update) | async-done | bytes 2097168 | tf_op jit(solution)/shard_map/all_gather | solution.py:113
  183.3 3.9 copy.67
  187.3 3.1 multiply_reduce_fusion.11
  196.8 47.5 %while.52 = (s32[]{:T(128)}, bf16[8,512,2,64]{1,3,2,0:T(8,128)(2,1)}, f32[8,2,512]{2,1,0:T(2,128)S(1)}, bf16[8,1024,64]{1,2,0:T(8,128)(2,1)}, pred[512,1024]{0,1...) while((s32[]{:T(128)}, ...), condition=%wide.region_8.9_spmd, body=%wide.region_5.0_spmd.sunk | while | flops 281082880 | bytes 14714977 | solution.py:201
  247.5 4.6 multiply_reduce_fusion.10
  253.1 47.7 %while.53 = (s32[]{:T(128)}, bf16[8,512,2,64]{1,3,2,0:T(8,128)(2,1)}, f32[8,2,512]{2,1,0:T(2,128)S(1)}, bf16[8,1024,64]{1,2,0:T(8,128)(2,1)}, pred[512,1024]{0,1...) while((s32[]{:T(128)}, ...), condition=%wide.region_18.19_spmd, body=%wide.region_15.18_spmd.sunk | while | flops 281082880 | bytes 14714977 | solution.py:201
  300.9 4.8 multiply_reduce_fusion.8
  306.0 19.1 all-gather.16.cloned.1.call-done
  325.1 11.0 fusion.226
  336.1 72.4 %all-gather.18.cloned.1.call-done = bf16[1024,4608]{1,0:T(8,128)(2,1)} async-done(((bf16[32,4608]{1,0:T(8,128)(2,1)}), bf16[1024,4608]{1,0:T(8,128)(2,1)}) %all-gather.18.cloned.1.call-update) | async-done | bytes 9437200 | tf_op jit(solution)/shard_map/all_gather | solution.py:119
  408.5 11.1 fusion.227
  419.6 72.4 %all-gather.20.cloned.1.call-done = bf16[4608,1024]{0,1:T(8,128)(2,1)} async-done(((bf16[4608,32]{0,1:T(8,128)(2,1)}), bf16[4608,1024]{0,1:T(8,128)(2,1)}) %all-gather.20.cloned.1.call-update) | async-done | bytes 9437200 | tf_op jit(solution)/shard_map/all_gather | solution.py:120
  492.1 17.0 multiply_convert_fusion.1
  509.1 9.2 fusion.230
  518.3 9.7 multiply_reduce_fusion.1
  528.1 11.4 fusion.228
  539.5 11.1 fusion.229
  550.6 17.1 multiply_convert_fusion
  567.7 9.2 fusion.233
  576.9 8.8 multiply_reduce_fusion
  597.5 108.8 %while.54 = (s32[]{:T(128)}, f32[8,512,2,64]{1,3,2,0:T(8,128)}, f32[8,1024,64]{1,2,0:T(8,128)}, f32[8,1024,64]{1,2,0:T(8,128)}, bf16[8,1024,64]{1,2,0:T(8,128)(2...) while((s32[]{:T(128)}, f32[8,512,2,64]{1,3,2,0:T(8,128)}, ...), condition=%wide.region_23.24_spmd, body=%wide.region_21.23_spmd.sunk | while | flops 686947328 | bytes 34767992 | solution.py:270
  706.4 3.9 convolution_convert_fusion
  719.5 103.1 %while.55 = (s32[]{:T(128)}, f32[8,512,2,64]{1,3,2,0:T(8,128)S(1)}, f32[8,1024,64]{1,2,0:T(8,128)}, f32[8,1024,64]{1,2,0:T(8,128)}, bf16[8,1024,64]{1,2,0:T(8,12...) while((s32[]{:T(128)}, f32[8,512,2,64]{1,3,2,0:T(8,128)S(1)}, ...), condition=%wide.region_30.31_spmd, body=%wide.region_28.30_spmd.sunk | while | flops 686947328 | bytes 34767992 | solution.py:270
  842.6 6.2 collective-permute-done.9
  864.8 3.6 convolution_add_fusion.3
  869.6 3.0 fusion.199
  872.7 3.3 convolution_add_fusion.2
  877.2 11.5 fusion.236
  888.7 14.1 convolution_add_fusion.1
  902.8 11.6 fusion.237
  914.5 14.2 convolution_add_fusion
  929.0 11.3 fusion.173
  940.2 14.4 add_bitcast_fusion
  954.6 18.7 copy.80
  974.0 9.5 fusion.163
  983.6 9.3 fusion.162
  1001.7 3.1 fusion.145
  1004.8 53.6 %all-reduce.12 = (f32[1024]{0:T(1024)S(1)}, f32[64]{0:T(128)}, f32[64]{0:T(128)}, f32[1024]{0:T(1024)S(1)}) all-reduce(f32[1024]{0:T(1024)S(1)} %add.355, f32[64]{0:T(128)S(1)} %add.349, f32[64]{0:T(128)S(1)} %add.350, f32[1024]{0:T(1024)S(1)} %add.360), channel_id=11, replica_groups=mesh['fsdp'=32] {'fsdp'}, use_global_device_ids=true, to_apply=%region_35.36.clone | all-reduce | flops 2176 | bytes 17408
  1059.6 4.1 fusion.167
  1065.2 54.5 %reduce-scatter.14.cloned.1.call-done = f32[32,512]{1,0:T(8,128)} async-done(((f32[1024,512]{1,0:T(8,128)}), f32[32,512]{1,0:T(8,128)}) %reduce-scatter.14.cloned.1.call-update) | async-done | bytes 65552 | tf_op jit(solution)/shard_map/reduce_scatter | solution.py:303
  1119.6 139.6 %reduce-scatter.10.cloned.1.call-done = f32[32,1024]{1,0:T(8,128)} async-done(((f32[1024,1024]{1,0:T(8,128)}), f32[32,1024]{1,0:T(8,128)}) %reduce-scatter.10.cloned.1.call-update) | async-done | bytes 131088 | tf_op jit(solution)/shard_map/reduce_scatter | solution.py:301
  1259.2 139.6 %reduce-scatter.16.cloned.1.call-done = f32[32,1024]{1,0:T(8,128)} async-done(((f32[1024,1024]{1,0:T(8,128)}), f32[32,1024]{1,0:T(8,128)}) %reduce-scatter.16.cloned.1.call-update) | async-done | bytes 131088 | tf_op jit(solution)/shard_map/reduce_scatter | solution.py:304
  1398.8 209.5 %reduce-scatter.18.cloned.1.call-done = f32[32,4608]{1,0:T(8,128)} async-done(((f32[1024,4608]{1,0:T(8,128)}), f32[32,4608]{1,0:T(8,128)}) %reduce-scatter.18.cloned.1.call-update) | async-done | bytes 589840 | tf_op jit(solution)/shard_map/reduce_scatter | solution.py:306
  1608.3 212.7 %reduce-scatter.20.cloned.1.call-done = f32[32,4608]{1,0:T(8,128)} async-done(((f32[1024,4608]{1,0:T(8,128)}), f32[32,4608]{1,0:T(8,128)}) %reduce-scatter.20.cloned.1.call-update) | async-done | bytes 589840 | tf_op jit(solution)/shard_map/reduce_scatter | solution.py:307
  1821.0 212.4 %reduce-scatter.22.cloned.1.call-done = f32[32,4608]{1,0:T(8,128)} async-done(((f32[1024,4608]{1,0:T(8,128)}), f32[32,4608]{1,0:T(8,128)}) %reduce-scatter.22.cloned.1.call-update) | async-done | bytes 589840
  (563 shorter events, 442.7 us)
Async XLA Ops:
  7.2 14.4 copy-start.107
  7.2 14.7 copy-start.108
  7.2 55.5 %copy-start.109 = (bf16[64]{0:T(256)(128)(2,1)S(1)}, bf16[64]{0:T(256)(128)(2,1)}, u32[]{:S(2)}) copy-start(bf16[64]{0:T(256)(128)(2,1)} %param.30) | copy-start | bytes 388
  7.2 56.0 %copy-start.110 = (bf16[64]{0:T(256)(128)(2,1)S(1)}, bf16[64]{0:T(256)(128)(2,1)}, u32[]{:S(2)}) copy-start(bf16[64]{0:T(256)(128)(2,1)} %param.29) | copy-start | bytes 388
  7.2 60.5 %all-gather.8.cloned.1.call-start = ((), (), s32[]{:S(2)}) async-start(), calls=%async_computation.7 | async-start | bytes 1081344 | tf_op jit(solution)/shard_map/all_gather | solution.py:115
  8.0 115.0 %all-gather.10.cloned.1.call-start = ((), (), s32[]{:S(2)}) async-start(), calls=%async_computation.8 | async-start | bytes 1081344 | tf_op jit(solution)/shard_map/all_gather | solution.py:114
  8.7 174.6 %all-gather.12.cloned.1.call-start = ((), (), s32[]{:S(2)}) async-start(), calls=%async_computation.9 | async-start | bytes 2162688 | tf_op jit(solution)/shard_map/all_gather | solution.py:113
  9.4 238.0 %all-gather.14.cloned.1.call-start = ((), (), s32[]{:S(2)}) async-start(), calls=%async_computation.10 | async-start | bytes 2162688 | tf_op jit(solution)/shard_map/all_gather | solution.py:116
  10.0 315.1 %all-gather.16.cloned.1.call-start = ((), (), s32[]{:S(2)}) async-start(), calls=%async_computation.11 | async-start | bytes 9732096 | tf_op jit(solution)/shard_map/all_gather | solution.py:118
  10.6 397.9 %all-gather.18.cloned.1.call-start = ((), (), s32[]{:S(2)}) async-start(), calls=%async_computation.12 | async-start | bytes 9732096 | tf_op jit(solution)/shard_map/all_gather | solution.py:119
  11.2 480.9 %all-gather.20.cloned.1.call-start = ((), (), s32[]{:S(2)}) async-start(), calls=%async_computation.13 | async-start | bytes 9732096 | tf_op jit(solution)/shard_map/all_gather | solution.py:120
  12.0 51.7 %collective-permute-start.4 = (bf16[512]{0:T(512)(128)(2,1)S(1)}, bf16[512]{0:T(512)(128)(2,1)S(1)}, u32[]{:S(2)}, u32[]{:S(2)}) collective-permute-start(bf16[512]{0:T(512)(128)(2,1)S(1)} %convert_element_type.317), channel_id=1, source_target_pairs={{0,1},{1,2},{2,3},{3,4},{4,5},{5,6},{6,7},{7,8},{8,9},{9,10},{10,1... | collective-permute-start | bytes 3080 | tf_op jit(solution)/shard_map/ppermute | solution.py:19
  14.4 50.1 %collective-permute-start.1 = (bf16[512]{0:T(512)(128)(2,1)S(1)}, bf16[512]{0:T(512)(128)(2,1)S(1)}, u32[]{:S(2)}, u32[]{:S(2)}) collective-permute-start(bf16[512]{0:T(512)(128)(2,1)S(1)} %convert_element_type.295), channel_id=1, source_target_pairs={{0,1},{1,2},{2,3},{3,4},{4,5},{5,6},{6,7},{7,8},{8,9},{9,10},{10,1... | collective-permute-start | bytes 3080 | tf_op jit(solution)/shard_map/ppermute | solution.py:19
  18.9 1046.2 %reduce-scatter.12.cloned.1.call-start = ((), (), s32[]{:S(2)}) async-start(), calls=%async_computation.15 | async-start | bytes 2162688 | tf_op jit(solution)/shard_map/reduce_scatter | solution.py:302
  21.5 42.2 %copy-start.94 = (f32[512]{0:T(512)}, f32[512]{0:T(512)S(1)}, u32[]{:S(2)}) copy-start(f32[512]{0:T(512)S(1)} %get-tuple-element.264) | copy-start | bytes 6148
  21.5 42.2 %copy-start.96 = (f32[512]{0:T(512)}, f32[512]{0:T(512)S(1)}, u32[]{:S(2)}) copy-start(f32[512]{0:T(512)S(1)} %get-tuple-element.265) | copy-start | bytes 6148
  21.6 46.2 %copy-start.4 = (bf16[2,512,1024]{2,1,0:T(8,128)(2,1)S(1)}, bf16[2,512,1024]{2,1,0:T(8,128)(2,1)}, u32[]{:S(2)}) copy-start(bf16[2,512,1024]{2,1,0:T(8,128)(2,1)} %param.22) | copy-start | bytes 6291460
  21.6 168.8 %copy-start.90 = (f32[512]{0:T(512)}, f32[512]{0:T(512)S(1)}, u32[]{:S(2)}) copy-start(f32[512]{0:T(512)S(1)} %fusion.215) | copy-start | bytes 6148
  62.6 127.8 %copy-start.78 = (f32[1024]{0:T(1024)}, f32[1024]{0:T(1024)S(1)}, u32[]{:S(2)}) copy-start(f32[1024]{0:T(1024)S(1)} %convert_element_type.292) | copy-start | bytes 12292
  62.6 124.6 %copy-start.92 = (f32[512]{0:T(512)}, f32[512]{0:T(512)S(1)}, u32[]{:S(2)}) copy-start(f32[512]{0:T(512)S(1)} %fusion.213) | copy-start | bytes 6148
  67.7 126.5 %copy-start.61 = (f32[512,32]{0,1:T(8,128)}, f32[512,32]{0,1:T(8,128)S(1)}, u32[]{:S(2)}) copy-start(f32[512,32]{0,1:T(8,128)S(1)} %get-tuple-element.415) | copy-start | bytes 196612
  67.7 126.6 %copy-start.63 = (f32[512,32]{0,1:T(8,128)}, f32[512,32]{0,1:T(8,128)S(1)}, u32[]{:S(2)}) copy-start(f32[512,32]{0,1:T(8,128)S(1)} %get-tuple-element.416) | copy-start | bytes 196612
  67.7 176.6 %copy-start.57 = (f32[512,32]{0,1:T(8,128)}, f32[512,32]{0,1:T(8,128)S(1)}, u32[]{:S(2)}) copy-start(f32[512,32]{0,1:T(8,128)S(1)} %get-tuple-element.419) | copy-start | bytes 196612
  67.7 176.6 %copy-start.59 = (f32[512,32]{0,1:T(8,128)}, f32[512,32]{0,1:T(8,128)S(1)}, u32[]{:S(2)}) copy-start(f32[512,32]{0,1:T(8,128)S(1)} %get-tuple-element.420) | copy-start | bytes 196612
  70.6 73.4 %collective-permute-start.3 = (bf16[512,512]{1,0:T(8,128)(2,1)}, bf16[512,512]{1,0:T(8,128)(2,1)}, u32[]{:S(2)}, u32[]{:S(2)}) collective-permute-start(bf16[512,512]{1,0:T(8,128)(2,1)} %convolution_convert_fusion.2), channel_id=1, source_target_pairs={{0,1},{1,2},{2,3},{3,4},{4,5},{5,6},{6,7},{7,8},{8,9},{9,10},{10,1... | collective-permute-start | bytes 1572872 | tf_op jit(solution)/shard_map/ppermute | solution.py:19
  130.9 22.2 %collective-permute-start.5 = (bf16[512,512]{0,1:T(8,128)(2,1)}, bf16[512,512]{0,1:T(8,128)(2,1)}, u32[]{:S(2)}, u32[]{:S(2)}) collective-permute-start(bf16[512,512]{0,1:T(8,128)(2,1)} %bitcast.73), channel_id=1, source_target_pairs={{0,1},{1,2},{2,3},{3,4},{4,5},{5,6},{6,7},{7,8},{8,9},{9,10},{10,1... | collective-permute-start | bytes 1572872 | tf_op jit(solution)/shard_map/ppermute | solution.py:19
  135.5 13.1 collective-permute-start
  139.6 15.8 collective-permute-start.2
  305.9 102.5 %copy-start.15 = (bf16[512,1024]{1,0:T(8,128)(2,1)}, bf16[512,1024]{1,0:T(8,128)(2,1)S(1)}, u32[]{:S(2)}) copy-start(bf16[512,1024]{1,0:T(8,128)(2,1)S(1)} %multiply_convert_fusion.5) | copy-start | bytes 3145732
  336.1 156.0 %copy-start.29 = (bf16[2,512,1024]{2,1,0:T(8,128)(2,1)S(1)}, bf16[2,512,1024]{2,1,0:T(8,128)(2,1)}, u32[]{:S(2)}) copy-start(bf16[2,512,1024]{2,1,0:T(8,128)(2,1)} %param.35) | copy-start | bytes 6291460
  528.1 11.4 copy-start.40
  587.0 119.4 %copy-start.12 = (f32[512,1024]{1,0:T(8,128)}, f32[512,1024]{1,0:T(8,128)S(1)}, u32[]{:S(2)}) copy-start(f32[512,1024]{1,0:T(8,128)S(1)} %get-tuple-element.369) | copy-start | bytes 6291460
  714.6 112.1 %collective-permute-start.6 = (bf16[512,512]{0,1:T(8,128)(2,1)}, bf16[512,512]{0,1:T(8,128)(2,1)S(1)}, u32[]{:S(2)}, u32[]{:S(2)}) collective-permute-start(bf16[512,512]{0,1:T(8,128)(2,1)} %bitcast.94), channel_id=1, source_target_pairs={{1,0},{2,1},{3,2},{4,3},{5,4},{6,5},{7,6},{8,7},{9,8},{10,9},{11,1... | collective-permute-start | bytes 1572872 | tf_op jit(solution)/shard_map/ppermute | solution.py:19
  825.4 4.4 collective-permute-start.8
  836.6 283.0 %reduce-scatter.14.cloned.1.call-start = ((), (), s32[]{:S(2)}) async-start(), calls=%async_computation.16 | async-start | bytes 2162688 | tf_op jit(solution)/shard_map/reduce_scatter | solution.py:303
  838.1 10.6 collective-permute-start.9
  840.9 11.1 collective-permute-start.7
  855.4 403.8 %reduce-scatter.10.cloned.1.call-start = ((), (), s32[]{:S(2)}) async-start(), calls=%async_computation.14 | async-start | bytes 4325376 | tf_op jit(solution)/shard_map/reduce_scatter | solution.py:301
  868.4 530.4 %reduce-scatter.16.cloned.1.call-start = ((), (), s32[]{:S(2)}) async-start(), calls=%async_computation.17 | async-start | bytes 4325376 | tf_op jit(solution)/shard_map/reduce_scatter | solution.py:304
  876.0 732.3 %reduce-scatter.18.cloned.1.call-start = ((), (), s32[]{:S(2)}) async-start(), calls=%async_computation.18 | async-start | bytes 19464192 | tf_op jit(solution)/shard_map/reduce_scatter | solution.py:306
  877.2 11.5 copy-start.41
  902.8 918.2 %reduce-scatter.20.cloned.1.call-start = ((), (), s32[]{:S(2)}) async-start(), calls=%async_computation.19 | async-start | bytes 19464192 | tf_op jit(solution)/shard_map/reduce_scatter | solution.py:307
  902.8 11.6 copy-start.42
  928.7 1104.6 %reduce-scatter.22.cloned.1.call-start = ((), (), s32[]{:S(2)}) async-start(), calls=%async_computation.20 | async-start | bytes 19464192
  928.9 11.3 copy-start.31
  974.0 9.6 copy-start.25
  1001.7 57.9 %copy-start.95 = (f32[512]{0:T(512)S(1)}, f32[512]{0:T(512)}, u32[]{:S(2)}) copy-start(f32[512]{0:T(512)} %copy-done.94) | copy-start | bytes 6148
  1001.7 57.9 %copy-start.97 = (f32[512]{0:T(512)S(1)}, f32[512]{0:T(512)}, u32[]{:S(2)}) copy-start(f32[512]{0:T(512)} %copy-done.96) | copy-start | bytes 6148
  (87 other events, 240.1 us)
Sparse Core Ops, SparseCore 0:
  10.9 56.4 all-gather.7
  70.2 52.6 all-gather.9
  125.8 57.4 all-gather.11
  186.0 55.2 all-gather.13
  244.1 80.9 all-gather.15
  327.8 80.6 all-gather.17
  411.4 80.6 all-gather.19
  836.7 144.7 reduce-scatter.11
  984.5 135.0 reduce-scatter.13
  1122.3 136.8 reduce-scatter.9
  1262.1 136.6 reduce-scatter.15
  1405.6 202.6 reduce-scatter.17
  1615.3 205.6 reduce-scatter.19
  1827.8 205.5 reduce-scatter.21
where the time goes:
time: 2050 us; the launch traced here: 2040 us
  waiting for transfers between devices  1220 us (60%)
  matrix products  522 us (25%)
  blocking collectives  94.1 us (5%)
  other arithmetic  82.3 us (4%)
  local copies, waits for them, and re-layouts  76 us (4%)
  starting transfers between devices  24.7 us (1%)
    unnamed x15, waiting for transfers between devices  216 us
    reduce_scatter x1, waiting for transfers between devices, local(): lax.psum_scatter(grad_up_w, 'fsdp', scatter_dimension=0, tiled=True)  213 us
    reduce_scatter x1, waiting for transfers between devices, local(): lax.psum_scatter(grad_gate_w, 'fsdp', scatter_dimension=0, tiled=True)  209 us
    reduce_scatter x1, waiting for transfers between devices, local(): lax.psum_scatter(grad_query_w, 'fsdp', scatter_dimension=0, tiled=True)  140 us
    reduce_scatter x1, waiting for transfers between devices, local(): lax.psum_scatter(grad_output_t, 'fsdp', scatter_dimension=0, tiled=True)  140 us
    dot_general x14, matrix products, rows_product(): lax.dot_general(left_rows, right_rows, (((0,), (0,)), ((), ())), preferre...  94.8 us
    unnamed x2, blocking collectives  94.1 us
    dot_general x14, matrix products, cols_product(): lax.dot_general(left_rows, right_rows, (((1,), (1,)), ((), ())), preferre...  85.1 us
  transfers between devices with their start and end apart: 24, of which 14 were waited for; matrix products, arithmetic and copies ran while one was open for 22% of the time, Pallas kernels for 0%

commit v1 on v0

--- a/solution.py
+++ b/solution.py
@@ -1,11 +1,434 @@
+import functools
 import math
 
 import jax
 import jax.numpy as jnp
 from jax import lax
+from jax.experimental import pallas as pl
+from jax.experimental.pallas import tpu as pltpu
 from jax.sharding import PartitionSpec as P
 
 SEQ = 1024
+CHUNKS = 11
+WIDE = 768
+MESH = pl.DeviceIdType.MESH
+ALL = slice(None)
+F32 = jnp.float32
+BF16 = jnp.bfloat16
+PARTS = (
+    ("A", pl.ds(0, 48), pl.ds(0, 384)),
+    ("B", pl.ds(0, 48), pl.ds(384, 384)),
+    ("C", pl.ds(48, 16), pl.ds(0, 768)),
+)
+OUTWARD = {
+    "A": ("z0", "z1", "z2", "y", "x"),
+    "B": ("z0", "z1", "z2", "x", "y"),
+    "C": ("x", "y", "z0", "z1", "z2"),
+}
+INWARD = {
+    "A": ("x", "y", "z0", "z1", "z2"),
+    "B": ("y", "x", "z0", "z1", "z2"),
+    "C": ("z0", "z1", "z2", "y", "x"),
+}
+SUM_SLOTS = 7
+LAND_SLOTS = 3
+
+
+def place():
+    me = lax.axis_index("fsdp")
+    return me, me // 8, (me // 4) % 2, (me // 2) % 2, me % 2
+
+
+def guarded(condition, action):
+    if condition is None:
+        action()
+    else:
+        pl.when(condition)(action)
+
+
+def greet(me, z):
+    gate = pltpu.get_barrier_semaphore()
+    for bit in (1, 2, 4):
+        pl.semaphore_signal(gate, inc=1, device_id=(me ^ bit,), device_id_type=MESH)
+
+    @pl.when(z > 0)
+    def _():
+        pl.semaphore_signal(gate, inc=1, device_id=(me - 8,), device_id_type=MESH)
+
+    @pl.when(z < 3)
+    def _():
+        pl.semaphore_signal(gate, inc=1, device_id=(me + 8,), device_id_type=MESH)
+
+    pl.semaphore_wait(gate, 3 + (z > 0).astype(jnp.int32) + (z < 3).astype(jnp.int32))
+
+
+class Gather:
+    def __init__(self, full, sent, landed):
+        self.full, self.sent, self.landed = full, sent, landed
+        self.me, self.z, self.y, self.x, self.core = place()
+
+    def moves(self, part, step, chunk):
+        kind, rows, columns = PARTS[part]
+        z, y, x, me = self.z, self.y, self.x, self.me
+
+        def view(zz, yy, xx):
+            return self.full.at[chunk, zz, yy, xx, rows, columns]
+
+        axis = OUTWARD[kind][step]
+        if axis[0] == "z":
+            far = int(axis[1])
+            yy, xx = (ALL, ALL) if kind == "C" else (y, x)
+            return (
+                ((z >= far) & (z < 3), z - far, me + 8, z >= far + 1, z - 1 - far),
+                ((z <= 3 - far) & (z > 0), z + far, me - 8, z <= 2 - far, z + 1 + far),
+            ), lambda zz: view(zz, yy, xx)
+        zz = z if kind == "C" else ALL
+        if axis == "y":
+            xx = x if kind == "A" else ALL
+            return ((None, y, me ^ 4, None, 1 - y),), lambda yy: view(zz, yy, xx)
+        yy = ALL if kind == "A" else y
+        return ((None, x, me ^ 2, None, 1 - x),), lambda xx: view(zz, yy, xx)
+
+    def copy(self, ref, device, part, step, chunk, way):
+        return pltpu.make_async_remote_copy(
+            src_ref=ref,
+            dst_ref=ref,
+            send_sem=self.sent.at[chunk, part, step, way],
+            recv_sem=self.landed.at[chunk, part, step, way],
+            device_id=(device,),
+            device_id_type=MESH,
+        )
+
+    def send(self, part, step, chunk):
+        moves, view = self.moves(part, step, chunk)
+        for way, (sends, mine, device, _, _) in enumerate(moves):
+            guarded(
+                sends,
+                lambda: self.copy(view(mine), device, part, step, chunk, way).start(),
+            )
+
+    def receive(self, part, step, chunk):
+        moves, view = self.moves(part, step, chunk)
+        for way, (_, _, _, receives, other) in enumerate(moves):
+            guarded(
+                receives,
+                lambda: self.copy(view(other), self.me ^ 2, part, step, chunk, way).wait_recv(),
+            )
+
+    def finish(self, part, step, chunk):
+        moves, view = self.moves(part, step, chunk)
+        for way, (sends, mine, device, _, _) in enumerate(moves):
+            guarded(
+                sends,
+                lambda: self.copy(view(mine), device, part, step, chunk, way).wait_send(),
+            )
+
+    def tick(self, time):
+        for step in range(6):
+            chunk = time - step
+
+            @pl.when((chunk >= 0) & (chunk < CHUNKS))
+            def _():
+                for part in range(len(PARTS)):
+                    if step > 0:
+                        self.receive(part, step - 1, chunk)
+                    if step < 5:
+                        self.send(part, step, chunk)
+
+    def drain(self):
+        def body(chunk, carry):
+            for part in range(len(PARTS)):
+                for step in range(5):
+                    self.finish(part, step, chunk)
+            return carry
+
+        lax.fori_loop(0, CHUNKS, body, 0)
+
+
+class Scatter:
+    def __init__(self, sums, lands, totals, sent, landed):
+        self.sums, self.lands, self.totals = sums, lands, totals
+        self.sent, self.landed = sent, landed
+        self.me, self.z, self.y, self.x, self.core = place()
+
+    def moves(self, part, step, chunk):
+        kind, rows, columns = PARTS[part]
+        z, y, x, me = self.z, self.y, self.x, self.me
+        slot, land = lax.rem(chunk, SUM_SLOTS), lax.rem(chunk, LAND_SLOTS)
+        first, second, up, down = self.lands[part]
+        axis = INWARD[kind][step]
+
+        def view(zz, yy, xx):
+            return self.sums.at[slot, zz, yy, xx, rows, columns]
+
+        if axis[0] == "z":
+            far = int(axis[1])
+            count = 3 - far
+            yy, xx = (ALL, ALL) if kind == "C" else (y, x)
+            above, below = pl.ds(far + 1, count), pl.ds(0, count)
+            up_land, down_land = up.at[land, pl.ds(far, count)], down.at[land, pl.ds(0, count)]
+            return (
+                (z == far, view(above, yy, xx), up_land, me + 8, z == far + 1, view(above, yy, xx)),
+                (z == 3 - far, view(below, yy, xx), down_land, me - 8, z == 2 - far, view(below, yy, xx)),
+            )
+        zz = z if kind == "C" else ALL
+        ref = (first if step == 0 or (kind == "C" and step == 3) else second).at[land]
+        if axis == "x":
+            yy = ALL if kind == "A" else y
+            return ((None, view(zz, yy, 1 - x), ref, me ^ 2, None, view(zz, yy, x)),)
+        xx = x if kind == "A" else ALL
+        return ((None, view(zz, 1 - y, xx), ref, me ^ 4, None, view(zz, y, xx)),)
+
+    def copy(self, source, target, device, part, step, chunk, way):
+        return pltpu.make_async_remote_copy(
+            src_ref=source,
+            dst_ref=target,
+            send_sem=self.sent.at[chunk, part, step, way],
+            recv_sem=self.landed.at[chunk, part, step, way],
+            device_id=(device,),
+            device_id_type=MESH,
+        )
+
+    def step(self, part, step, chunk):
+        if step > 0:
+            for way, move in enumerate(self.moves(part, step - 1, chunk)):
+                sends, source, land, device, receives, target = move
+
+                def add():
+                    self.copy(land, land, self.me ^ 2, part, step - 1, chunk, way).wait_recv()
+                    target[...] = (target[...].astype(F32) + land[...].astype(F32)).astype(BF16)
+
+                guarded(receives, add)
+                guarded(
+                    sends,
+                    lambda: self.copy(source, land, device, part, step - 1, chunk, way).wait_send(),
+                )
+        if step < 5:
+            for way, move in enumerate(self.moves(part, step, chunk)):
+                sends, source, land, device, _, _ = move
+                guarded(
+                    sends,
+                    lambda: self.copy(source, land, device, part, step, chunk, way).start(),
+                )
+        else:
+            _, rows, columns = PARTS[part]
+            slot = lax.rem(chunk, SUM_SLOTS)
+            self.totals[chunk, rows, columns] = self.sums[
+                slot, self.z, self.y, self.x, rows, columns
+            ].astype(F32)
+
+    def tick(self, time, ready):
+        for step in range(5, -1, -1):
+            chunk = time - step
+
+            @pl.when((chunk >= 0) & (chunk < CHUNKS))
+            def _():
+                if step == 0:
+                    ready(chunk)
+                for part in range(len(PARTS)):
+                    self.step(part, step, chunk)
+
+
+def pair_rows(core):
+    mine = pl.ds(pl.multiple_of(core * 32, 32), 32)
+    other = pl.ds(pl.multiple_of((1 - core) * 32, 32), 32)
+    return mine, other
+
+
+def gather_kernel(w_ref, o_ref, full, local_sem, pair_sent, pair_landed, sent, landed):
+    me, z, y, x, core = place()
+    greet(me, z)
+    mine, other = pair_rows(core)
+
+    def to_pair(rows):
+        return pltpu.make_async_remote_copy(
+            src_ref=w_ref.at[1 - core],
+            dst_ref=full.at[:, z, y, x, rows, :],
+            send_sem=pair_sent,
+            recv_sem=pair_landed,
+            device_id=(me ^ 1,),
+            device_id_type=MESH,
+        )
+
+    own = pltpu.make_async_copy(w_ref.at[core], full.at[:, z, y, x, mine, :], local_sem)
+    own.start()
+    to_pair(mine).start()
+    own.wait()
+    to_pair(mine).wait_send()
+    to_pair(other).wait_recv()
+    gather = Gather(full, sent, landed)
+
+    def body(time, carry):
+        gather.tick(time)
+        return carry
+
+    lax.fori_loop(0, CHUNKS + 5, body, 0)
+    gather.drain()
+    out = pltpu.make_async_copy(full, o_ref, local_sem)
+    out.start()
+    out.wait()
+
+
+def scatter_kernel(d_ref, o_ref, sums, *rest):
+    lands = (rest[0:4], rest[4:8], rest[8:12])
+    totals, load_sem, pair_sent, pair_landed, sent, landed = rest[12:]
+    me, z, y, x, core = place()
+    greet(me, z)
+    mine, other = pair_rows(core)
+    scatter = Scatter(sums, lands, totals, sent, landed)
+
+    def load(chunk):
+        return pltpu.make_async_copy(
+            d_ref.at[chunk], sums.at[lax.rem(chunk, SUM_SLOTS)], load_sem.at[lax.rem(chunk, 2)]
+        )
+
+    load(0).start()
+
+    def ready(chunk):
+        @pl.when(chunk + 1 < CHUNKS)
+        def _():
+            load(chunk + 1).start()
+
+        load(chunk).wait()
+
+    def body(time, carry):
+        scatter.tick(time, ready)
+        return carry
+
+    lax.fori_loop(0, CHUNKS + 5, body, 0)
+
+    def to_pair(half):
+        return pltpu.make_async_remote_copy(
+            src_ref=totals.at[:, other, :],
+            dst_ref=o_ref.at[half],
+            send_sem=pair_sent,
+            recv_sem=pair_landed,
+            device_id=(me ^ 1,),
+            device_id_type=MESH,
+        )
+
+    own = pltpu.make_async_copy(totals.at[:, mine, :], o_ref.at[core], load_sem.at[0])
+    own.start()
+    to_pair(core).start()
+    to_pair(core).wait_send()
+    to_pair(1 - core).wait_recv()
+    own.wait()
+
+
+def semaphores():
+    return [pltpu.SemaphoreType.DMA((CHUNKS, len(PARTS), 5, 2))] * 2
+
+
+def land_shapes():
+    slots = LAND_SLOTS
+    plain = [(slots, 4, 2, 48, 384), (slots, 4, 48, 384), (slots, 3, 48, 384), (slots, 3, 48, 384)]
+    late = [(slots, 2, 16, 768), (slots, 16, 768), (slots, 3, 2, 2, 16, 768), (slots, 3, 2, 2, 16, 768)]
+    return [pltpu.VMEM(shape, BF16) for shape in plain + plain + late]
+
+
+def params(number):
+    return pltpu.CompilerParams(
+        collective_id=number, has_side_effects=True, vmem_limit_bytes=60 * 2**20
+    )
+
+
+def pair_swap(block):
+    return lax.ppermute(block, "fsdp", [(i, i ^ 1) for i in range(lax.axis_size("fsdp"))])
+
+
+def gather_grid(w_query, w_key, w_value, w_output, w_gate, w_up, w_down):
+    rows = w_query.shape[0]
+    halves = [
+        jnp.stack(jnp.split(w, 2, axis=1)) for w in (w_query, w_key, w_value, w_output.T)
+    ]
+    first = jnp.concatenate(halves[:2], axis=2)[:, None]
+    second = jnp.concatenate(halves[2:], axis=2)[:, None]
+    wide = jnp.concatenate(
+        [w.reshape(rows, 2, CHUNKS - 2, 256).transpose(1, 2, 0, 3) for w in (w_gate, w_up, w_down.T)],
+        axis=3,
+    )
+    packed = jnp.concatenate([first, second, wide], axis=1)
+    full = pl.pallas_call(
+        gather_kernel,
+        out_shape=jax.ShapeDtypeStruct((CHUNKS, 4, 2, 2, 64, WIDE), BF16),
+        in_specs=[pl.BlockSpec(memory_space=pl.ANY)],
+        out_specs=pl.BlockSpec(memory_space=pl.ANY),
+        scratch_shapes=[pltpu.VMEM((CHUNKS, 4, 2, 2, 64, WIDE), BF16)]
+        + [pltpu.SemaphoreType.DMA] * 3
+        + semaphores(),
+        compiler_params=params(0),
+        name="gather",
+    )(packed)
+    full = full.reshape(CHUNKS, 1024, WIDE)
+    other = pair_swap(full)
+    core = lax.axis_index("fsdp") % 2
+    low, high = jnp.where(core == 0, full, other), jnp.where(core == 0, other, full)
+
+    def both(chunk, start, stop):
+        return jnp.concatenate([low[chunk, :, start:stop], high[chunk, :, start:stop]], axis=1)
+
+    def wide_of(start):
+        parts = [half[2:, :, start : start + 256].transpose(1, 0, 2).reshape(1024, -1) for half in (low, high)]
+        return jnp.concatenate(parts, axis=1)
+
+    return (
+        both(0, 0, 512),
+        both(0, 512, 768),
+        both(1, 0, 256),
+        both(1, 256, 768).T,
+        wide_of(0),
+        wide_of(256),
+        wide_of(512).T,
+    )
+
+
+def scatter_all(sums):
+    attn_gain, w_query, w_key, w_value, w_output, ffn_gain, w_gate, w_up, w_down = sums
+    halves = [jnp.stack(jnp.split(w, 2, axis=1)) for w in (w_query, w_key, w_value, w_output)]
+    first = jnp.concatenate(halves[:2], axis=2)[:, None]
+    second = jnp.concatenate(halves[2:], axis=2)[:, None]
+    wide = jnp.concatenate(
+        [w.reshape(1024, 2, CHUNKS - 2, 256).transpose(1, 2, 0, 3) for w in (w_gate, w_up, w_down)],
+        axis=3,
+    )
+    packed = jnp.concatenate([first, second, wide], axis=1)
+    core = lax.axis_index("fsdp") % 2
+    other = pair_swap(packed[1 - core].astype(BF16))
+    terms = (packed[core] + other.astype(F32)).astype(BF16)
+    out = pl.pallas_call(
+        scatter_kernel,
+        out_shape=jax.ShapeDtypeStruct((2, CHUNKS, 32, WIDE), F32),
+        in_specs=[pl.BlockSpec(memory_space=pl.ANY)],
+        out_specs=pl.BlockSpec(memory_space=pl.ANY),
+        scratch_shapes=[pltpu.VMEM((SUM_SLOTS, 4, 2, 2, 64, WIDE), BF16)]
+        + land_shapes()
+        + [pltpu.VMEM((CHUNKS, 64, WIDE), F32), pltpu.SemaphoreType.DMA((2,))]
+        + [pltpu.SemaphoreType.DMA] * 2
+        + semaphores(),
+        compiler_params=params(1),
+        name="scatter",
+    )(terms.reshape(CHUNKS, 4, 2, 2, 64, WIDE))
+
+    def both(chunk, start, stop):
+        return jnp.concatenate([out[0, chunk, :, start:stop], out[1, chunk, :, start:stop]], axis=1)
+
+    def wide_of(start):
+        return out[:, 2:, :, start : start + 256].transpose(2, 0, 1, 3).reshape(32, -1)
+
+    def gain(term):
+        return lax.psum_scatter(term, "fsdp", scatter_dimension=0, tiled=True)
+
+    return (
+        gain(attn_gain),
+        both(0, 0, 512),
+        both(0, 512, 768),
+        both(1, 0, 256),
+        both(1, 256, 768),
+        gain(ffn_gain),
+        wide_of(0),
+        wide_of(256),
+        wide_of(512),
+    )
 
 
 EPS = 1e-05
@@ -326,9 +749,238 @@
     )
 
 
+def local_grid(
+    inputs,
+    segments,
+    attn_gain,
+    w_query,
+    key_projection,
+    value_projection,
+    w_output,
+    query_gain,
+    key_norm_gain,
+    ffn_gain,
+    w_gate,
+    w_up,
+    w_down,
+    cotangent,
+):
+    batches = inputs.shape[0]
+    tokens = inputs.shape[1]
+    head_width = query_gain.shape[0]
+    query_width = w_query.shape[1]
+    kv_width = key_projection.shape[1]
+    query_head_rows = query_width // head_width
+    kv_heads = kv_width // head_width
+    heads_per_group = query_head_rows // kv_heads
+    scale = 1.0 / math.sqrt(head_width)
+    query_gain_f = query_gain.astype(jnp.float32)
+    key_gain_f = key_norm_gain.astype(jnp.float32)
+    device_index = lax.axis_index("fsdp")
+    places_row = jnp.arange(tokens, dtype=jnp.int32)
+    causal = places_row[None, :] <= places_row[:, None]
+    same_run = device_index * tokens // SEQ == (device_index - 1) * tokens // SEQ
+    outputs_list = []
+    grads_list = []
+    shard_sums = None
+    gain_sums = None
+    gain_attn = lax.all_gather(attn_gain, "fsdp", axis=0, tiled=True)
+    gain_ffn = lax.all_gather(ffn_gain, "fsdp", axis=0, tiled=True)
+    full_query, full_key, full_value, full_output, full_gate, full_up, full_down = gather_grid(
+        w_query, key_projection, value_projection, w_output, w_gate, w_up, w_down
+    )
+    for batch_index in range(batches):
+        hidden = inputs[batch_index].astype(jnp.float32)
+        segment = segments[batch_index]
+        normed_f, norm_pull = jax.vjp(row_norm, hidden, gain_attn.astype(jnp.float32))
+        normed = normed_f.astype(jnp.bfloat16)
+        query_raw = plain_product(normed, full_query)
+        key_projected = plain_product(normed, full_key)
+        value_reduced = plain_product(normed, full_value).astype(jnp.bfloat16)
+        lower_count = jnp.sum((segment[None, :] < segment[:, None]).astype(jnp.int32), axis=1)
+        local_places = places_row - lower_count
+        cos_local, sin_local = angles(local_places, head_width)
+        key_sent = prepare_inputs(key_projected, key_gain_f, cos_local, sin_local, kv_heads).astype(
+            jnp.bfloat16
+        )
+        remote_key, remote_value, remote_segment = from_behind(
+            (key_sent, value_reduced, segment.astype(jnp.bfloat16)), "fsdp", 1
+        )
+        remote_match = (remote_segment.astype(jnp.int32)[None, :] == segment[:, None]) & same_run
+        places_all = local_places + jnp.sum(remote_match.astype(jnp.int32), axis=1)
+        cosine_table, sine_table_rows = angles(places_all, head_width)
+        query_f, query_pull = jax.vjp(
+            lambda raw_rows, gain_row: prepare_inputs(
+                raw_rows, gain_row, cosine_table, sine_table_rows, query_head_rows
+            ),
+            query_raw,
+            query_gain_f,
+        )
+        key_f, key_pull = jax.vjp(
+            lambda raw_rows, gain_row: prepare_inputs(
+                raw_rows, gain_row, cosine_table, sine_table_rows, kv_heads
+            ),
+            key_projected,
+            key_gain_f,
+        )
+        query_low = query_f.astype(jnp.bfloat16)
+        key_low = key_f.astype(jnp.bfloat16)
+        allowed = jnp.concatenate(
+            [remote_match, causal & (segment[None, :] == segment[:, None])], axis=1
+        )
+        query_split = query_low.reshape(tokens, kv_heads, heads_per_group, head_width).transpose(
+            1, 0, 2, 3
+        )
+        key_split = (
+            jnp.concatenate([remote_key, key_low], axis=0)
+            .reshape(2 * tokens, kv_heads, head_width)
+            .transpose(1, 0, 2)
+        )
+        value_split = (
+            jnp.concatenate([remote_value, value_reduced], axis=0)
+            .reshape(2 * tokens, kv_heads, head_width)
+            .transpose(1, 0, 2)
+        )
+
+        def head_forward(blocks):
+            query_part, key_part, value_part = blocks
+            scores = (
+                jnp.einsum("tgd,ld->gtl", query_part, key_part, preferred_element_type=jnp.float32)
+                * scale
+            )
+            scores = jnp.where(allowed[None], scores, NEG)
+            row_peak = jnp.max(scores, axis=-1, keepdims=True)
+            raised = jnp.exp(scores - row_peak)
+            row_total = jnp.sum(raised, axis=-1, keepdims=True)
+            prob_rows = (raised / row_total).astype(jnp.bfloat16)
+            mixed_part = jnp.einsum(
+                "gtl,ld->tgd", prob_rows, value_part, preferred_element_type=jnp.float32
+            )
+            return (mixed_part.astype(jnp.bfloat16), (row_peak + jnp.log(row_total))[..., 0])
+
+        mixed_split, log_totals = lax.map(head_forward, (query_split, key_split, value_split))
+        attn_mix = mixed_split.transpose(1, 0, 2, 3).reshape(tokens, query_width)
+        attended = hidden + plain_product(attn_mix, full_output)
+        ffn_f, ffn_pull = jax.vjp(row_norm, attended, gain_ffn.astype(jnp.float32))
+        ffn_in = ffn_f.astype(jnp.bfloat16)
+        gate_raw = plain_product(ffn_in, full_gate)
+        upward = plain_product(ffn_in, full_up)
+        active_f, active_pull = jax.vjp(silu_product, gate_raw, upward)
+        active = active_f.astype(jnp.bfloat16)
+        result = attended + plain_product(active, full_down)
+        outputs_list.append(result.astype(jnp.bfloat16))
+        grad_result = cotangent[batch_index]
+        grad_down_t = rows_product(grad_result, active)
+        grad_active = cols_product(grad_result, full_down)
+        grad_gate_f, grad_up_f = active_pull(grad_active)
+        grad_gate_low = grad_gate_f.astype(jnp.bfloat16)
+        grad_up_low = grad_up_f.astype(jnp.bfloat16)
+        grad_gate_w = rows_product(ffn_in, grad_gate_low)
+        grad_up_w = rows_product(ffn_in, grad_up_low)
+        grad_ffn_in = cols_product(grad_gate_low, full_gate) + cols_product(grad_up_low, full_up)
+        grad_attended_norm, grad_ffn_gain = ffn_pull(grad_ffn_in)
+        grad_attended = grad_result.astype(jnp.float32) + grad_attended_norm
+        grad_branch = grad_attended.astype(jnp.bfloat16)
+        grad_output_t = rows_product(grad_branch, attn_mix)
+        grad_mixed = cols_product(grad_branch, full_output).astype(jnp.bfloat16)
+        grad_split = grad_mixed.reshape(tokens, kv_heads, heads_per_group, head_width).transpose(
+            1, 0, 2, 3
+        )
+
+        def head_backward(blocks):
+            query_part, key_part, value_part, grad_part, log_part = blocks
+            scores = (
+                jnp.einsum("tgd,ld->gtl", query_part, key_part, preferred_element_type=jnp.float32)
+                * scale
+            )
+            scores = jnp.where(allowed[None], scores, NEG)
+            prob_rows = jnp.exp(scores - log_part[..., None])
+            grad_probs = jnp.einsum(
+                "tgd,ld->gtl", grad_part, value_part, preferred_element_type=jnp.float32
+            )
+            center = jnp.sum(prob_rows * grad_probs, axis=-1, keepdims=True)
+            grad_scores = (prob_rows * (grad_probs - center)).astype(jnp.bfloat16)
+            grad_query_part = (
+                jnp.einsum("gtl,ld->tgd", grad_scores, key_part, preferred_element_type=jnp.float32)
+                * scale
+            )
+            grad_key_part = (
+                jnp.einsum(
+                    "gtl,tgd->ld", grad_scores, query_part, preferred_element_type=jnp.float32
+                )
+                * scale
+            )
+            grad_value_part = jnp.einsum(
+                "gtl,tgd->ld",
+                prob_rows.astype(jnp.bfloat16),
+                grad_part,
+                preferred_element_type=jnp.float32,
+            )
+            return (grad_query_part, grad_key_part, grad_value_part)
+
+        grad_query_split, grad_key_split, grad_value_split = lax.map(
+            head_backward, (query_split, key_split, value_split, grad_split, log_totals)
+        )
+        grad_query_rot = grad_query_split.transpose(1, 0, 2, 3).reshape(tokens, query_width)
+        grad_key_all = grad_key_split.transpose(1, 0, 2).reshape(2 * tokens, kv_width)
+        grad_value_all = grad_value_split.transpose(1, 0, 2).reshape(2 * tokens, kv_width)
+        back_key_grad, back_value_grad = (
+            from_behind(grad_key_all[:tokens].astype(jnp.bfloat16), "fsdp", -1).astype(jnp.float32),
+            from_behind(grad_value_all[:tokens].astype(jnp.bfloat16), "fsdp", -1).astype(
+                jnp.float32
+            ),
+        )
+        grad_key_rot = grad_key_all[tokens:] + back_key_grad
+        grad_value_low = (grad_value_all[tokens:] + back_value_grad).astype(jnp.bfloat16)
+        grad_query_raw, grad_query_gain = query_pull(grad_query_rot)
+        grad_key_raw, grad_key_gain = key_pull(grad_key_rot)
+        grad_query_low = grad_query_raw.astype(jnp.bfloat16)
+        grad_key_low = grad_key_raw.astype(jnp.bfloat16)
+        grad_query_w = rows_product(normed, grad_query_low)
+        grad_key_w = rows_product(normed, grad_key_low)
+        grad_value_w = rows_product(normed, grad_value_low)
+        grad_normed = (
+            cols_product(grad_query_low, full_query)
+            + cols_product(grad_key_low, full_key)
+            + cols_product(grad_value_low, full_value)
+        )
+        grad_hidden_norm, grad_attn_gain = norm_pull(grad_normed)
+        grads_list.append((grad_attended + grad_hidden_norm).astype(jnp.bfloat16))
+        gain_sums = add_sets(gain_sums, (grad_query_gain, grad_key_gain))
+        shard_terms = (
+            grad_attn_gain,
+            grad_query_w,
+            grad_key_w,
+            grad_value_w,
+            grad_output_t,
+            grad_ffn_gain,
+            grad_gate_w,
+            grad_up_w,
+            grad_down_t,
+        )
+        shard_sums = add_sets(shard_sums, shard_terms)
+    shard_sums = scatter_all(shard_sums)
+    head_sums = lax.psum((gain_sums[0], gain_sums[1]), "fsdp")
+    return (
+        jnp.stack(outputs_list),
+        jnp.stack(grads_list),
+        shard_sums[0],
+        shard_sums[1],
+        shard_sums[2],
+        shard_sums[3],
+        shard_sums[4].T,
+        head_sums[0],
+        head_sums[1],
+        shard_sums[5],
+        shard_sums[6],
+        shard_sums[7],
+        shard_sums[8].T,
+    )
+
+
 def solution(mesh):
     return jax.shard_map(
-        local,
+        local_grid if mesh.shape["fsdp"] == 32 else local,
         mesh=mesh,
         in_specs=(
             P(None, "fsdp", None),

time: 2050 us -> 1310 us (0.64)
  waiting for transfers between devices: 1220 us -> 0.03 us
  Pallas kernels: 0 us -> 293 us
  local copies, waits for them, and re-layouts: 76 us -> 195 us
  other arithmetic: 82.3 us -> 172 us
    reduce_scatter x6 -> x0, waiting for transfers between devices: 756 us -> none  [the longest x1 213 us: local(): lax.psum_scatter(grad_up_w, 'fsdp', scatter_dimension=0, tiled=True)]
    pallas_call x0 -> x2, Pallas kernels: none -> 293 us  [the longest x1 149 us: gather_grid(): pl.pallas_call(gather_kernel, out_shape=jax.ShapeDtypeStruct((CHUNKS, 4,...]
    all_gather x7 -> x0, waiting for transfers between devices: 240 us -> none  [the longest x1 72.4 us: local(): lax.all_gather(w_down, 'fsdp', axis=1, tiled=True)]
    unnamed x15 -> x0, waiting for transfers between devices: 216 us -> none
    concatenate x6 -> x13, other arithmetic: 9.04 us -> 57.7 us  [the longest x1 45.3 us: scatter_all(): packed = jnp.concatenate([first, second, wide], axis=1)]
    convert_element_type x2 -> x4, local copies, waits for them, and re-layouts: 4.57 us -> 45.1 us  [the longest x1 22.6 us: scatter_all(): terms = (packed[core] + other.astype(F32)).astype(BF16)]
    add x0 -> x2, local copies, waits for them, and re-layouts: none -> 37.5 us  [add_sets(): former + latter]
    reshape x0 -> x10, local copies, waits for them, and re-layouts: none -> 27.5 us  [the longest x1 22.7 us: gather_grid(): full = full.reshape(CHUNKS, 1024, WIDE)]
  transfers between devices with their start and end apart: 24 -> 12, of which waited for: 14 -> 0; matrix products, arithmetic and copies ran while one was open for 22% -> 17% of each run, Pallas kernels for 0% -> 0%
where the time goes in v1:
time: 1310 us; the launch traced here: 1300 us
  matrix products  515 us (39%)
  Pallas kernels  293 us (22%)
  local copies, waits for them, and re-layouts  195 us (15%)
  other arithmetic  172 us (13%)
  blocking collectives  92 us (7%)
  starting transfers between devices  25.4 us (2%)
    pallas_call x1, Pallas kernels, gather_grid(): pl.pallas_call(gather_kernel, out_shape=jax.ShapeDtypeStruct((CHUNKS, 4,...  149 us
    pallas_call x1, Pallas kernels, scatter_all(): pl.pallas_call(scatter_kernel, out_shape=jax.ShapeDtypeStruct((2, CHUNKS,...  144 us
    dot_general x14, matrix products, plain_product(): return jnp.dot(left_rows, right_rows, preferred_element_type=jnp.float32)  97.5 us
    unnamed x2, blocking collectives  92 us
    dot_general x14, matrix products, rows_product(): lax.dot_general(left_rows, right_rows, (((0,), (0,)), ((), ())), preferre...  86.8 us
    dot_general x14, matrix products, cols_product(): lax.dot_general(left_rows, right_rows, (((1,), (1,)), ((), ())), preferre...  67.6 us
    dot_general x16, matrix products, head_forward(): jnp.einsum('gtl,ld->tgd', prob_rows, value_part, preferred_element_type=j...  47.8 us
    dot_general x16, matrix products, head_backward(): jnp.einsum('gtl,tgd->ld', prob_rows.astype(jnp.bfloat16), grad_part, pref...  46.8 us
  transfers between devices with their start and end apart: 12, of which 0 were waited for; matrix products, arithmetic and copies ran while one was open for 17% of the time, Pallas kernels for 0%

profile of v1, /device:TPU:0, one launch (start us, length us, event | category | flops | bytes accessed | tf_op | source)
XLA Modules:
  0.0 1296.7 jit_solution(13066837947564577702)
XLA Ops:
  6.9 148.6 %gather.1 = bf16[11,4,2,2,64,768]{5,4,3,2,1,0:T(8,128)(2,1)} custom-call(bf16[2,11,32,768]{3,2,1,0:T(8,128)(2,1)} %maximum_maximum_fusion.1.w_ref), custom_call_target="tpu_custom_call" | custom-call | tf_op jit(solution)/shard_map/gather/pallas_call | solution.py:351
  155.6 22.7 %copy.88 = bf16[11,1024,768]{1,2,0:T(8,128)(2,1)} copy(bf16[11,1024,768]{2,1,0:T(8,128)(2,1)} %bitcast.718) | data formatting | bytes 34603008 | tf_op jit(solution)/shard_map/reshape | solution.py:362
  184.9 52.3 %all-reduce.13 = (bf16[1024]{0:T(1024)(128)(2,1)S(1)}, bf16[1024]{0:T(1024)(128)(2,1)S(1)}) all-reduce(bf16[1024]{0:T(1024)(128)(2,1)S(1)} %dynamic-update-slice, bf16[1024]{0:T(1024)(128)(2,1)S(1)} %dynamic-update-slice.1), channel_id=1, replica_groups=mesh['fsdp'=32] {'fsdp'}, use_global_device_ids=true, to_apply=%add.8 | all-reduce | flops 2048 | bytes 8192
  240.4 17.9 %broadcast_select_fusion.1 = (bf16[11,1024,768]{1,2,0:T(8,128)(2,1)}, bf16[11,1024,768]{1,2,0:T(8,128)(2,1)S(1)}) fusion(bf16[11,1024,768]{1,2,0:T(8,128)(2,1)} %copy.88, bf16[11,1024,768]{1,2,0:T(8,128)(2,1)} %collective-permute-done, pred[]{:T(512)S(6)} %eq.19), kind=kLoop, calls=%fused_computation.136 | loop fusion | flops 17301504 | bytes 69206016 | tf_op jit(solution)/shard_map/jit(_where)/select_n | solution.py:365
  264.7 3.0 slice_bitcast_fusion.9
  267.7 10.2 fusion.239
  279.2 5.7 fusion.240
  288.9 9.2 fusion.179
  298.1 9.1 fusion.174
  308.5 5.7 collective-permute-start.4
  319.3 3.3 collective-permute-start.6
  336.5 47.5 %while.52 = (s32[]{:T(128)}, bf16[8,512,2,64]{1,3,2,0:T(8,128)(2,1)}, f32[8,2,512]{2,1,0:T(2,128)S(1)}, bf16[8,1024,64]{1,2,0:T(8,128)(2,1)}, pred[512,1024]{0,1...) while((s32[]{:T(128)}, ...), condition=%wide.region_8.9_spmd, body=%wide.region_5.8_spmd.sunk | while | flops 281082880 | bytes 14714977 | solution.py:861
  357.2 3.0 fusion.327
  392.1 47.7 %while.53 = (s32[]{:T(128)}, bf16[8,512,2,64]{1,3,2,0:T(8,128)(2,1)}, f32[8,2,512]{2,1,0:T(2,128)S(1)}, bf16[8,1024,64]{1,2,0:T(8,128)(2,1)}, pred[512,1024]{0,1...) while((s32[]{:T(128)}, ...), condition=%wide.region_18.19_spmd, body=%wide.region_15.18_spmd.sunk | while | flops 281082880 | bytes 14714977 | solution.py:861
  430.7 3.0 fusion.331
  439.9 4.6 multiply_reduce_fusion.8
  446.2 13.3 %fusion.224 = f32[512,4608]{1,0:T(8,128)} fusion(bf16[512,1024]{1,0:T(8,128)(2,1)S(1)} %multiply_convert_fusion.3, bf16[1024,2304]{0,1:T(8,128)(2,1)} %bitcast.762, bf16[1024,2304]{0,1:T(8,128)(2,1)} %bitcast.754), kind=kOutput, calls=%fused_computation.434 | convolution fusion | flops 4850712576 | bytes 19922944 | tf_op jit(solution)/shard_map/dot_general | solution.py:473
  459.5 19.6 %fusion.124 = (bf16[512,4608]{1,0:T(8,128)(2,1)}, bf16[512,4608]{1,0:T(8,128)(2,1)}, bf16[512,4608]{1,0:T(8,128)(2,1)}) fusion(f32[512,4608]{1,0:T(8,128)} %fusion.224, f32[4608,512]{0,1:T(8,128)} %fusion.179, bf16[512,1024]{1,0:T(8,128)(2,1)S(1)} %multiply_convert_fusion.3, bf16[1024,2304]{0,1:T(8,128)(2,1)} %bitcast.758, bf16[1024,2304]{0,1:T(8,128)(2,1)S(1)} %bitcast.751), kind=kOutput, calls=%fused_computation.141 | convolution fusion | flops 4888461312 | bytes 43515904 | tf_op jit(solution)/shard_map/dot_general | solution.py:473
  479.1 9.1 fusion.222
  488.3 9.3 multiply_reduce_fusion.1
  497.6 12.8 fusion.223
  510.4 19.5 %fusion.127 = (bf16[512,4608]{1,0:T(8,128)(2,1)}, bf16[512,4608]{1,0:T(8,128)(2,1)}, bf16[512,4608]{1,0:T(8,128)(2,1)}) fusion(f32[512,4608]{1,0:T(8,128)} %fusion.223, f32[4608,512]{0,1:T(8,128)} %fusion.174, bf16[512,1024]{1,0:T(8,128)(2,1)S(1)} %get-tuple-element.390, bf16[1024,2304]{0,1:T(8,128)(2,1)} %bitcast.760, bf16[1024,2304]{0,1:T(8,128)(2,1)S(1)} %bitcast.753), kind=kOutput, calls=%fused_computation.144 | convolution fusion | flops 4888461312 | bytes 43515904 | tf_op jit(solution)/shard_map/dot_general | solution.py:473
  529.9 9.1 fusion.221
  539.1 9.2 multiply_reduce_fusion
  560.3 102.8 %while.55 = (s32[]{:T(128)}, f32[8,512,2,64]{1,3,2,0:T(8,128)}, f32[8,1024,64]{1,2,0:T(8,128)}, f32[8,1024,64]{1,2,0:T(8,128)}, bf16[8,1024,64]{1,2,0:T(8,128)(2...) while((s32[]{:T(128)}, f32[8,512,2,64]{1,3,2,0:T(8,128)}, ...), condition=%wide.region_30.31_spmd, body=%wide.region_28.30_spmd.sunk | while | flops 686947328 | bytes 34767992 | solution.py:921
  678.8 108.4 %while.54 = (s32[]{:T(128)}, f32[8,512,2,64]{1,3,2,0:T(8,128)}, f32[8,1024,64]{1,2,0:T(8,128)}, f32[8,1024,64]{1,2,0:T(8,128)}, bf16[8,1024,64]{1,2,0:T(8,128)(2...) while((s32[]{:T(128)}, f32[8,512,2,64]{1,3,2,0:T(8,128)}, ...), condition=%wide.region_23.24_spmd, body=%wide.region_21.23_spmd.sunk | while | flops 686947328 | bytes 34767992 | solution.py:921
  795.1 11.7 fusion.242
  806.8 9.3 fusion.243
  833.8 3.3 fusion.191
  837.1 14.7 %convolution_add_fusion.1 = f32[1024,4608]{1,0:T(8,128)} fusion(f32[1024,4608]{1,0:T(8,128)} %fusion.243, bf16[512,1024]{1,0:T(8,128)(2,1)S(1)} %copy-done.38, bf16[512,4608]{1,0:T(8,128)(2,1)} %get-tuple-element.319), kind=kOutput, calls=%fused_computation.161 | convolution fusion | flops 4836556800 | bytes 43515904 | tf_op jit(solution)/shard_map/dot_general | solution.py:477
  851.9 11.6 fusion.177
  863.5 3.4 convolution_add_fusion.4
  866.8 12.9 convolution_add_fusion
  879.7 14.1 %convolution_add_fusion.2 = f32[1024,4608]{1,0:T(8,128)} fusion(f32[1024,4608]{1,0:T(8,128)} %fusion.242, bf16[512,1024]{1,0:T(8,128)(2,1)S(1)} %copy-done.38, bf16[512,4608]{1,0:T(8,128)(2,1)} %get-tuple-element.318), kind=kOutput, calls=%fused_computation.162 | convolution fusion | flops 4836556800 | bytes 43515904 | tf_op jit(solution)/shard_map/dot_general | solution.py:477
  893.8 18.7 %copy.96 = f32[1024,4608]{0,1:T(8,128)} copy(f32[1024,4608]{1,0:T(8,128)} %convolution_add_fusion.2) | data formatting | bytes 37748736 | tf_op jit(solution)/shard_map/add | solution.py:495
  912.5 18.8 %copy.97 = f32[1024,4608]{0,1:T(8,128)} copy(f32[1024,4608]{1,0:T(8,128)} %convolution_add_fusion.1) | data formatting | bytes 37748736 | tf_op jit(solution)/shard_map/add | solution.py:495
  947.5 5.6 maximum_bitcast_fusion
  953.1 45.3 %maximum_maximum_fusion = f32[2,11,1024,768]{2,3,1,0:T(8,128)} fusion(f32[2,9,1024,256]{2,3,1,0:T(8,128)} %bitcast.715, f32[2,9,1024,256]{2,3,1,0:T(8,128)} %bitcast.717, f32[2,9,1024,256]{2,3,1,0:T(8,128)} %bitcast.716, f32[2,1,1024,768]{2,3,1,0:T(8,128)} %get-tuple-element.445, f32[2,1,1024,768]{2,3,1,0:T(8,128)} %get-tuple-element.444), kind=kLoop, calls=%fused_computation.130 | loop fusion | flops 69206016 | bytes 138412032 | tf_op jit(solution)/shard_map/concatenate | solution.py:394
  998.5 18.0 %fusion.121 = bf16[11,1024,768]{1,2,0:T(8,128)(2,1)} fusion(f32[2,11,1024,768]{2,3,1,0:T(8,128)} %maximum_maximum_fusion, s32[]{:T(128)S(6)} %select_n.54), kind=kLoop, calls=%fused_computation.134 | loop fusion | bytes 34603012 | tf_op jit(solution)/shard_map/convert_element_type | solution.py:396
  1016.5 3.0 collective-permute-start.11
  1019.6 9.5 fusion.166
  1029.1 9.2 fusion.167
  1046.7 3.1 fusion.149
  1049.8 39.8 %all-reduce.12 = (f32[1024]{0:T(1024)S(1)}, f32[64]{0:T(128)}, f32[64]{0:T(128)}, f32[1024]{0:T(1024)S(1)}) all-reduce(f32[1024]{0:T(1024)S(1)} %add.331, f32[64]{0:T(128)S(1)} %add.343, f32[64]{0:T(128)S(1)} %add.344, f32[1024]{0:T(1024)S(1)} %add.345), channel_id=2, replica_groups=mesh['fsdp'=32] {'fsdp'}, use_global_device_ids=true, to_apply=%region_36.37.clone | all-reduce | flops 2176 | bytes 17408
  1090.7 4.0 fusion.171
  1096.3 23.4 %fusion.120 = bf16[11,1024,768]{1,2,0:T(8,128)(2,1)} fusion(bf16[11,1024,768]{1,2,0:T(8,128)(2,1)} %collective-permute-done.11, f32[2,11,1024,768]{2,3,1,0:T(8,128)} %maximum_maximum_fusion, s32[]{:T(128)S(6)} %select_n.53), kind=kLoop, calls=%fused_computation.132 | loop fusion | flops 25952256 | bytes 69206016 | tf_op jit(solution)/shard_map/convert_element_type | solution.py:397
  1119.6 22.6 %copy.100 = bf16[11,1024,768]{2,1,0:T(8,128)(2,1)} copy(bf16[11,1024,768]{1,2,0:T(8,128)(2,1)} %fusion.120) | data formatting | bytes 34603008 | tf_op jit(solution)/shard_map/convert_element_type | solution.py:397
  1142.2 144.4 %scatter.1 = f32[2,11,32,768]{3,2,1,0:T(8,128)} custom-call(bf16[11,4,2,2,64,768]{5,4,3,2,1,0:T(8,128)(2,1)} %bitcast.719), custom_call_target="tpu_custom_call" | custom-call | tf_op jit(solution)/shard_map/scatter/pallas_call | solution.py:398
  (608 shorter events, 446.3 us)
Async XLA Ops:
  155.5 22.8 %copy-start.115 = (s32[2,512]{1,0:T(2,128)S(1)}, s32[2,512]{1,0:T(2,128)}, u32[]{:S(2)}) copy-start(s32[2,512]{1,0:T(2,128)} %param.23) | copy-start | bytes 12292
  155.6 27.7 %copy-start.118 = (bf16[64]{0:T(256)(128)(2,1)S(1)}, bf16[64]{0:T(256)(128)(2,1)}, u32[]{:S(2)}) copy-start(bf16[64]{0:T(256)(128)(2,1)} %param.29) | copy-start | bytes 388
  155.6 27.7 %copy-start.119 = (bf16[64]{0:T(256)(128)(2,1)S(1)}, bf16[64]{0:T(256)(128)(2,1)}, u32[]{:S(2)}) copy-start(bf16[64]{0:T(256)(128)(2,1)} %param.30) | copy-start | bytes 388
  155.6 27.8 %copy-start.120 = (bf16[32]{0:T(256)(128)(2,1)S(1)}, bf16[32]{0:T(256)(128)(2,1)}, u32[]{:S(2)}) copy-start(bf16[32]{0:T(256)(128)(2,1)} %param.24) | copy-start | bytes 196
  155.6 28.0 %copy-start.121 = (bf16[32]{0:T(256)(128)(2,1)S(1)}, bf16[32]{0:T(256)(128)(2,1)}, u32[]{:S(2)}) copy-start(bf16[32]{0:T(256)(128)(2,1)} %param.31) | copy-start | bytes 196
  155.6 28.2 %copy-start.2 = (bf16[2,512,1024]{2,1,0:T(8,128)(2,1)S(1)}, bf16[2,512,1024]{2,1,0:T(8,128)(2,1)}, u32[]{:S(2)}) copy-start(bf16[2,512,1024]{2,1,0:T(8,128)(2,1)} %param.22) | copy-start | bytes 6291460
  178.3 62.0 %collective-permute-start = (bf16[11,1024,768]{1,2,0:T(8,128)(2,1)}, bf16[11,1024,768]{1,2,0:T(8,128)(2,1)}, u32[]{:S(2)}, u32[]{:S(2)}) collective-permute-start(bf16[11,1024,768]{1,2,0:T(8,128)(2,1)} %copy.88), channel_id=1, source_target_pairs={{0,1},{1,0},{2,3},{3,2},{4,5},{5,4},{6,7},{7,6},{8,9},{9,8},{10,11... | collective-permute-start | bytes 51904520 | tf_op jit(solution)/shard_map/ppermute | solution.py:336
  178.4 59.4 %collective-permute-start.2 = (bf16[512]{0:T(512)(128)(2,1)S(1)}, bf16[512]{0:T(512)(128)(2,1)S(1)}, u32[]{:S(2)}, u32[]{:S(2)}) collective-permute-start(bf16[512]{0:T(512)(128)(2,1)S(1)} %convert_element_type.307), channel_id=1, source_target_pairs={{0,1},{1,2},{2,3},{3,4},{4,5},{5,6},{6,7},{7,8},{8,9},{9,10},{10,1... | collective-permute-start | bytes 3080 | tf_op jit(solution)/shard_map/ppermute | solution.py:442
  180.8 57.0 %collective-permute-start.5 = (bf16[512]{0:T(512)(128)(2,1)S(1)}, bf16[512]{0:T(512)(128)(2,1)S(1)}, u32[]{:S(2)}, u32[]{:S(2)}) collective-permute-start(bf16[512]{0:T(512)(128)(2,1)S(1)} %convert_element_type.329), channel_id=1, source_target_pairs={{0,1},{1,2},{2,3},{3,4},{4,5},{5,6},{6,7},{7,8},{8,9},{9,10},{10,1... | collective-permute-start | bytes 3080 | tf_op jit(solution)/shard_map/ppermute | solution.py:442
  183.3 139.3 %copy-start.111 = (f32[64]{0:T(128)}, f32[64]{0:T(128)S(1)}, u32[]{:S(2)}) copy-start(f32[64]{0:T(128)S(1)} %convert_element_type.319) | copy-start | bytes 772
  183.3 130.9 %copy-start.109 = (f32[64]{0:T(128)}, f32[64]{0:T(128)S(1)}, u32[]{:S(2)}) copy-start(f32[64]{0:T(128)S(1)} %convert_element_type.312) | copy-start | bytes 772
  184.3 52.9 %copy-start.105 = (f32[512]{0:T(512)}, f32[512]{0:T(512)S(1)}, u32[]{:S(2)}) copy-start(f32[512]{0:T(512)S(1)} %get-tuple-element.225) | copy-start | bytes 6148
  184.4 102.2 %copy-start.103 = (f32[512]{0:T(512)}, f32[512]{0:T(512)S(1)}, u32[]{:S(2)}) copy-start(f32[512]{0:T(512)S(1)} %fusion.217) | copy-start | bytes 6148
  184.9 100.2 %copy-start.101 = (f32[512]{0:T(512)}, f32[512]{0:T(512)S(1)}, u32[]{:S(2)}) copy-start(f32[512]{0:T(512)S(1)} %fusion.219) | copy-start | bytes 6148
  237.2 49.3 %copy-start.93 = (f32[1024]{0:T(1024)}, f32[1024]{0:T(1024)S(1)}, u32[]{:S(2)}) copy-start(f32[1024]{0:T(1024)S(1)} %convert_element_type.304) | copy-start | bytes 12292
  240.3 83.3 %copy-start.67 = (f32[512,32]{0,1:T(8,128)}, f32[512,32]{0,1:T(8,128)S(1)}, u32[]{:S(2)}) copy-start(f32[512,32]{0,1:T(8,128)S(1)} %get-tuple-element.419) | copy-start | bytes 196612
  240.4 83.3 %copy-start.69 = (f32[512,32]{0,1:T(8,128)}, f32[512,32]{0,1:T(8,128)S(1)}, u32[]{:S(2)}) copy-start(f32[512,32]{0,1:T(8,128)S(1)} %get-tuple-element.420) | copy-start | bytes 196612
  240.4 86.5 %copy-start.63 = (f32[512,32]{0,1:T(8,128)}, f32[512,32]{0,1:T(8,128)S(1)}, u32[]{:S(2)}) copy-start(f32[512,32]{0,1:T(8,128)S(1)} %get-tuple-element.423) | copy-start | bytes 196612
  240.4 86.5 %copy-start.65 = (f32[512,32]{0,1:T(8,128)}, f32[512,32]{0,1:T(8,128)S(1)}, u32[]{:S(2)}) copy-start(f32[512,32]{0,1:T(8,128)S(1)} %get-tuple-element.424) | copy-start | bytes 196612
  263.8 50.4 %copy-start.98 = (f32[512,8]{0,1:T(8,128)}, f32[512,8]{0,1:T(8,128)S(1)}, u32[]{:S(2)}) copy-start(f32[512,8]{0,1:T(8,128)S(1)} %get-tuple-element.429) | copy-start | bytes 49156
  263.8 50.5 %copy-start.13 = (f32[512,8,64]{0,2,1:T(8,128)}, f32[512,8,64]{0,2,1:T(8,128)S(1)}, u32[]{:S(2)}) copy-start(f32[512,8,64]{0,2,1:T(8,128)S(1)} %get-tuple-element.430) | copy-start | bytes 3145732
  264.6 49.6 %copy-start.96 = (f32[512,8]{0,1:T(8,128)}, f32[512,8]{0,1:T(8,128)S(1)}, u32[]{:S(2)}) copy-start(f32[512,8]{0,1:T(8,128)S(1)} %get-tuple-element.427) | copy-start | bytes 49156
  264.7 49.6 %copy-start.15 = (f32[512,8,64]{0,2,1:T(8,128)}, f32[512,8,64]{0,2,1:T(8,128)S(1)}, u32[]{:S(2)}) copy-start(f32[512,8,64]{0,2,1:T(8,128)S(1)} %get-tuple-element.428) | copy-start | bytes 3145732
  267.7 17.2 %copy-start.44 = (bf16[1024,512]{0,1:T(8,128)(2,1)}, bf16[1024,512]{0,1:T(8,128)(2,1)S(1)}, u32[]{:S(2)}) copy-start(bf16[1024,512]{0,1:T(8,128)(2,1)S(1)} %get-tuple-element.328) | copy-start | bytes 3145732
  277.9 20.2 %copy-start.34 = (bf16[9,1024,256]{1,2,0:T(8,128)(2,1)}, bf16[9,1024,256]{1,2,0:T(8,128)(2,1)S(1)}, u32[]{:S(2)}) copy-start(bf16[9,1024,256]{1,2,0:T(8,128)(2,1)S(1)} %get-tuple-element.321) | copy-start | bytes 14155780
  286.5 36.0 %copy-start.89 = (f32[512,16]{0,1:T(8,128)}, f32[512,16]{0,1:T(8,128)S(1)}, u32[]{:S(2)}) copy-start(f32[512,16]{0,1:T(8,128)S(1)} %get-tuple-element.433) | copy-start | bytes 98308
  286.5 36.1 %copy-start.4 = (f32[512,16,64]{0,2,1:T(8,128)}, f32[512,16,64]{0,2,1:T(8,128)S(1)}, u32[]{:S(2)}) copy-start(f32[512,16,64]{0,2,1:T(8,128)S(1)} %get-tuple-element.434) | copy-start | bytes 6291460
  287.9 34.6 %copy-start.91 = (f32[512,16]{0,1:T(8,128)}, f32[512,16]{0,1:T(8,128)S(1)}, u32[]{:S(2)}) copy-start(f32[512,16]{0,1:T(8,128)S(1)} %get-tuple-element.431) | copy-start | bytes 98308
  288.0 34.7 %copy-start.6 = (f32[512,16,64]{0,2,1:T(8,128)}, f32[512,16,64]{0,2,1:T(8,128)S(1)}, u32[]{:S(2)}) copy-start(f32[512,16,64]{0,2,1:T(8,128)S(1)} %get-tuple-element.432) | copy-start | bytes 6291460
  307.2 21.1 %collective-permute-start.1 = (bf16[512,512]{1,0:T(8,128)(2,1)}, bf16[512,512]{1,0:T(8,128)(2,1)S(1)}, u32[]{:S(2)}, u32[]{:S(2)}) collective-permute-start(bf16[512,512]{1,0:T(8,128)(2,1)} %convolution_convert_fusion.3), channel_id=1, source_target_pairs={{0,1},{1,2},{2,3},{3,4},{4,5},{5,6},{6,7},{7,8},{8,9},{9,10},{10,1... | collective-permute-start | bytes 1572872 | tf_op jit(solution)/shard_map/ppermute | solution.py:442
  308.5 75.5 %collective-permute-start.4 = (bf16[512,512]{1,0:T(8,128)(2,1)}, bf16[512,512]{1,0:T(8,128)(2,1)}, u32[]{:S(2)}, u32[]{:S(2)}) collective-permute-start(bf16[512,512]{1,0:T(8,128)(2,1)} %convolution_convert_fusion.2), channel_id=1, source_target_pairs={{0,1},{1,2},{2,3},{3,4},{4,5},{5,6},{6,7},{7,8},{8,9},{9,10},{10,1... | collective-permute-start | bytes 1572872 | tf_op jit(solution)/shard_map/ppermute | solution.py:442
  316.0 17.0 %collective-permute-start.3 = (bf16[512,512]{0,1:T(8,128)(2,1)}, bf16[512,512]{0,1:T(8,128)(2,1)}, u32[]{:S(2)}, u32[]{:S(2)}) collective-permute-start(bf16[512,512]{0,1:T(8,128)(2,1)} %bitcast.76), channel_id=1, source_target_pairs={{0,1},{1,2},{2,3},{3,4},{4,5},{5,6},{6,7},{7,8},{8,9},{9,10},{10,1... | collective-permute-start | bytes 1572872 | tf_op jit(solution)/shard_map/ppermute | solution.py:442
  319.3 69.5 %collective-permute-start.6 = (bf16[512,512]{0,1:T(8,128)(2,1)}, bf16[512,512]{0,1:T(8,128)(2,1)}, u32[]{:S(2)}, u32[]{:S(2)}) collective-permute-start(bf16[512,512]{0,1:T(8,128)(2,1)} %bitcast.110), channel_id=1, source_target_pairs={{0,1},{1,2},{2,3},{3,4},{4,5},{5,6},{6,7},{7,8},{8,9},{9,10},{10,1... | collective-permute-start | bytes 1572872 | tf_op jit(solution)/shard_map/ppermute | solution.py:442
  445.9 102.4 %copy-start.26 = (f32[512,1024]{1,0:T(8,128)}, f32[512,1024]{1,0:T(8,128)S(1)}, u32[]{:S(2)}) copy-start(f32[512,1024]{1,0:T(8,128)S(1)} %get-tuple-element.436) | copy-start | bytes 6291460
  549.6 244.1 %copy-start.8 = (f32[512,1024]{1,0:T(8,128)}, f32[512,1024]{1,0:T(8,128)S(1)}, u32[]{:S(2)}) copy-start(f32[512,1024]{1,0:T(8,128)S(1)} %get-tuple-element.360) | copy-start | bytes 6291460
  822.4 111.5 %collective-permute-start.7 = (bf16[512,512]{0,1:T(8,128)(2,1)}, bf16[512,512]{0,1:T(8,128)(2,1)S(1)}, u32[]{:S(2)}, u32[]{:S(2)}) collective-permute-start(bf16[512,512]{0,1:T(8,128)(2,1)} %bitcast.133), channel_id=1, source_target_pairs={{1,0},{2,1},{3,2},{4,3},{5,4},{6,5},{7,6},{8,7},{9,8},{10,9},{11,1... | collective-permute-start | bytes 1572872 | tf_op jit(solution)/shard_map/ppermute | solution.py:442
  823.7 115.6 %collective-permute-start.8 = (bf16[512,512]{0,1:T(8,128)(2,1)}, bf16[512,512]{0,1:T(8,128)(2,1)}, u32[]{:S(2)}, u32[]{:S(2)}) collective-permute-start(bf16[512,512]{0,1:T(8,128)(2,1)} %bitcast.138), channel_id=1, source_target_pairs={{1,0},{2,1},{3,2},{4,3},{5,4},{6,5},{7,6},{8,7},{9,8},{10,9},{11,1... | collective-permute-start | bytes 1572872 | tf_op jit(solution)/shard_map/ppermute | solution.py:442
  825.0 109.3 %collective-permute-start.9 = (bf16[512,512]{0,1:T(8,128)(2,1)}, bf16[512,512]{0,1:T(8,128)(2,1)S(1)}, u32[]{:S(2)}, u32[]{:S(2)}) collective-permute-start(bf16[512,512]{0,1:T(8,128)(2,1)} %bitcast.153), channel_id=1, source_target_pairs={{1,0},{2,1},{3,2},{4,3},{5,4},{6,5},{7,6},{8,7},{9,8},{10,9},{11,1... | collective-permute-start | bytes 1572872 | tf_op jit(solution)/shard_map/ppermute | solution.py:442
  826.3 110.7 %collective-permute-start.10 = (bf16[512,512]{0,1:T(8,128)(2,1)}, bf16[512,512]{0,1:T(8,128)(2,1)}, u32[]{:S(2)}, u32[]{:S(2)}) collective-permute-start(bf16[512,512]{0,1:T(8,128)(2,1)} %bitcast.158), channel_id=1, source_target_pairs={{1,0},{2,1},{3,2},{4,3},{5,4},{6,5},{7,6},{8,7},{9,8},{10,9},{11,1... | collective-permute-start | bytes 1572872 | tf_op jit(solution)/shard_map/ppermute | solution.py:442
  832.7 30.7 %copy-start.49 = (bf16[512,16,64]{0,2,1:T(8,128)(2,1)}, bf16[512,16,64]{0,2,1:T(8,128)(2,1)S(1)}, u32[]{:S(2)}) copy-start(bf16[512,16,64]{0,2,1:T(8,128)(2,1)S(1)} %get-tuple-element.414) | copy-start | bytes 3145732
  837.1 29.7 %slice-start = ((s8[4718592]{0:T(1024)(128)(4,1)}), s8[4194304]{0:T(1024)(128)(4,1)S(1)}, s32[]{:S(2)}) async-start(s8[4718592]{0:T(1024)(128)(4,1)} %bitcast.720), calls=%async_computation | async-start | bytes 8388608
  998.5 21.1 %copy-start.113 = (f32[1024]{0:T(1024)S(1)}, f32[1024]{0:T(1024)}, u32[]{:S(2)}) copy-start(f32[1024]{0:T(1024)} %get-tuple-element.209) | copy-start | bytes 12292
  998.5 21.1 %copy-start.114 = (f32[1024]{0:T(1024)S(1)}, f32[1024]{0:T(1024)}, u32[]{:S(2)}) copy-start(f32[1024]{0:T(1024)} %get-tuple-element.207) | copy-start | bytes 12292
  998.5 21.1 %copy-start.116 = (f32[64]{0:T(128)S(1)}, f32[64]{0:T(128)}, u32[]{:S(2)}) copy-start(f32[64]{0:T(128)} %get-tuple-element.213) | copy-start | bytes 772
  998.5 21.1 %copy-start.117 = (f32[64]{0:T(128)S(1)}, f32[64]{0:T(128)}, u32[]{:S(2)}) copy-start(f32[64]{0:T(128)} %get-tuple-element.416) | copy-start | bytes 772
  1016.5 79.8 %collective-permute-start.11 = (bf16[11,1024,768]{1,2,0:T(8,128)(2,1)}, bf16[11,1024,768]{1,2,0:T(8,128)(2,1)}, u32[]{:S(2)}, u32[]{:S(2)}) collective-permute-start(bf16[11,1024,768]{1,2,0:T(8,128)(2,1)} %fusion.121), channel_id=1, source_target_pairs={{0,1},{1,0},{2,3},{3,2},{4,5},{5,4},{6,7},{7,6},{8,9},{9,8},{10,11... | collective-permute-start | bytes 51904520 | tf_op jit(solution)/shard_map/ppermute | solution.py:336
  1046.7 44.0 %copy-start.106 = (f32[512]{0:T(512)S(1)}, f32[512]{0:T(512)}, u32[]{:S(2)}) copy-start(f32[512]{0:T(512)} %copy-done.105) | copy-start | bytes 6148
  1046.7 44.0 %copy-start.108 = (f32[512]{0:T(512)S(1)}, f32[512]{0:T(512)}, u32[]{:S(2)}) copy-start(f32[512]{0:T(512)} %copy-done.107) | copy-start | bytes 6148
  (92 other events, 395.9 us)
